TPU v7x, 512 devices: a whole 4x8x8 slice. The times are simulated.
512 devices in a mesh: gx: 8 (over y), gy: 8 (over z), gz: 8 (over x, core).
Axes of the slice: x: 4, y: 8, z: 8, core: 2. Of those that a mesh axis runs over, the one named last changes fastest.
Arguments:
- divergence: float32 [128, 128, 1024], P('gz', 'gx', 'gy'), may hold values from -6 to 6
- pressure_prev: float32 [128, 128, 1024], P('gz', 'gx', 'gy'), may hold values from -6 to 6
Outputs:
- pressure: float32 [128, 128, 1024], P('gz', 'gx', 'gy')
- residual: float32 [128, 128, 1024], P('gz', 'gx', 'gy')
- coarse_correction: float32 [4, 4, 32], replicated
All inputs are finite; a program needn't handle non-finite values.
Results may differ from a plain program's by a relative error of at most 0.0004.
Values sent between devices are 32-bit elements; how exact they have to be, the bound alone decides.
A program may use at most 64 MiB of HBM per device.

v0:
```python
import jax
import jax.numpy as jnp
from jax import lax
from jax.sharding import PartitionSpec as P

LEVELS = 6


first_scale = 1.0 / 7.5
rho_one = 1.0 / (2.0 * (5.0 / 3.0) - 0.6)
carry_coef = 0.6 * rho_one
fresh_coef = 2.0 * rho_one / (0.75 * 6.0)


def extended(x, sides, width):
    for axis, dim in sides:
        peers, length = (lax.axis_size(axis), x.shape[dim])
        up = [(i, (i + 1) % peers) for i in range(peers - 1)]
        down = [(j, i) for i, j in up]
        last = lax.slice_in_dim(x, length - width, length, axis=dim)
        first = lax.slice_in_dim(x, 0, width, axis=dim)
        before = lax.ppermute(last, axis, up)
        after = lax.ppermute(first, axis, down)
        x = jnp.concatenate([before, x, after], axis=dim)
    return x


def stencil(values):
    padded = jnp.pad(values, 1)
    beside = padded[2:, 1:-1, 1:-1] + padded[:-2, 1:-1, 1:-1]
    beside = beside + padded[1:-1, 2:, 1:-1] + padded[1:-1, :-2, 1:-1]
    beside = beside + padded[1:-1, 1:-1, 2:] + padded[1:-1, 1:-1, :-2]
    return 6.0 * values - beside


def valid_op(padded):
    beside = padded[2:, 1:-1, 1:-1] + padded[:-2, 1:-1, 1:-1]
    beside = beside + padded[1:-1, 2:, 1:-1] + padded[1:-1, :-2, 1:-1]
    beside = beside + padded[1:-1, 1:-1, 2:] + padded[1:-1, 1:-1, :-2]
    return 6.0 * padded[1:-1, 1:-1, 1:-1] - beside


def local_stencil(values):
    padded = extended(values, (("gz", 0), ("gx", 1), ("gy", 2)), 1)
    return valid_op(padded)


def smooth_pass(iterate, source, apply_op, from_zero):
    residue = source if from_zero else source - apply_op(iterate)
    update = residue * first_scale
    iterate = update if from_zero else iterate + update
    residue = source - apply_op(iterate)
    update = carry_coef * update + fresh_coef * residue
    return iterate + update


def restrict(values):
    shape_a, shape_b, shape_c = values.shape
    blocks = values.reshape(shape_a // 2, 2, shape_b // 2, 2, shape_c // 2, 2)
    return 0.5 * jnp.sum(blocks, axis=(1, 3, 5))


def prolong(values):
    shape_a, shape_b, shape_c = values.shape
    spread = jnp.broadcast_to(
        values[:, None, :, None, :, None], (shape_a, 2, shape_b, 2, shape_c, 2)
    )
    return spread.reshape(2 * shape_a, 2 * shape_b, 2 * shape_c)


def vcycle(level_num, iterate, source):
    iterate = smooth_pass(iterate, source, stencil, True)
    coarsest = None
    if level_num < LEVELS - 1:
        residue = source - stencil(iterate)
        coarse, coarsest = vcycle(level_num + 1, None, restrict(residue))
        iterate = iterate + prolong(coarse)
    result = smooth_pass(iterate, source, stencil, False)
    if level_num == LEVELS - 1:
        coarsest = result
    return (result, coarsest)


def collect(values):
    gathered = lax.all_gather(values, "gz", axis=0, tiled=True)
    gathered = lax.all_gather(gathered, "gy", axis=2, tiled=True)
    return lax.all_gather(gathered, "gx", axis=1, tiled=True)


def own_block(whole, block_shape):
    start_z = lax.axis_index("gz") * block_shape[0]
    start_x = lax.axis_index("gx") * block_shape[1]
    start_y = lax.axis_index("gy") * block_shape[2]
    return lax.dynamic_slice(whole, (start_z, start_x, start_y), block_shape)


def body_cycle(level_num, iterate, source, from_zero, gather_at):
    if level_num == gather_at:
        whole_source = collect(source)
        coarse, coarsest = vcycle(level_num, None, whole_source)
        return (own_block(coarse, source.shape), coarsest)
    iterate = smooth_pass(iterate, source, local_stencil, from_zero)
    residue = source - local_stencil(iterate)
    coarse, coarsest = body_cycle(level_num + 1, None, restrict(residue), True, gather_at)
    iterate = iterate + prolong(coarse)
    return (smooth_pass(iterate, source, local_stencil, False), coarsest)


def body(divergence, pressure_prev):
    gather_at = 3
    pressure, coarse_correction = body_cycle(0, pressure_prev, divergence, False, gather_at)
    residual = divergence - local_stencil(pressure)
    return (pressure, residual, coarse_correction)


def solution(mesh):
    in_specs = (P("gz", "gx", "gy"), P("gz", "gx", "gy"))
    out_specs = (P("gz", "gx", "gy"), P("gz", "gx", "gy"), P())
    return jax.shard_map(body, mesh=mesh, in_specs=in_specs, out_specs=out_specs, check_vma=False)
```

profile of v0, /device:TPU:314, one launch (start us, length us, event | category | flops | bytes accessed | tf_op | source)
XLA Modules:
  0.0 486.1 jit_solution(2891422709954949127)
XLA Ops:
  3.3 3.6 collective-permute-start
  8.3 3.3 collective-permute-start.2
  12.9 4.2 collective-permute-done.3
  19.2 3.9 collective-permute-start.5
  23.1 3.5 collective-permute-done.4
  38.2 3.3 collective-permute-start.8
  42.9 4.2 collective-permute-done.9
  49.2 3.9 collective-permute-start.11
  66.2 3.3 collective-permute-start.14
  70.9 4.2 collective-permute-done.15
  77.2 3.9 collective-permute-start.17
  87.3 9.8 %reshape.41 = f32[8,2,8,2,64,2]{5,4,3,2,1,0:T(8,128)} reshape(f32[16,16,128]{2,1,0:T(8,128)S(1)} %fusion.54) | data formatting | bytes 262144 | tf_op jit(solution)/shard_map/reshape | solution.py:59
  97.1 4.0 reduce_sum.45
  108.0 3.6 collective-permute-start.20
  112.9 4.2 collective-permute-done.21
  119.1 3.9 collective-permute-start.23
  138.1 4.2 collective-permute-done.27
  144.4 3.9 collective-permute-start.29
  164.6 4.2 collective-permute-done.33
  170.8 3.9 collective-permute-start.35
  189.2 4.2 collective-permute-done.39
  195.3 3.9 collective-permute-start.41
  202.6 11.2 %all_gather.9 = f32[16,2,16]{2,1,0:T(2,128)S(1)} all-gather(f32[2,2,16]{2,1,0:T(2,128)S(1)} %broadcast_multiply_fusion.5), channel_id=1, replica_groups=mesh['gx'=8,'gy'=8,'gz'=8] {'gz'}, dimensions={0}, use_global_device_ids=true | all-gather | bytes 2304 | tf_op jit(solution)/shard_map/all_gather | solution.py:85
  213.8 24.6 %all_gather.10 = f32[16,2,128]{0,1,2:T(2,128)S(1)} all-gather(f32[16,2,16]{0,1,2:T(2,128)S(1)} %copy.5), channel_id=1, replica_groups=mesh['gx'=8,'gy'=8,'gz'=8] {'gy'}, dimensions={2}, use_global_device_ids=true | all-gather | bytes 18432 | tf_op jit(solution)/shard_map/all_gather | solution.py:86
  238.5 24.8 %all_gather.11 = f32[16,16,128]{2,0,1:T(8,128)S(1)} all-gather(f32[16,2,128]{2,0,1:T(8,128)S(1)} %copy.6), channel_id=1, replica_groups=mesh['gx'=8,'gy'=8,'gz'=8] {'gx'}, dimensions={1}, use_global_device_ids=true | all-gather | bytes 147456 | tf_op jit(solution)/shard_map/all_gather | solution.py:87
  263.6 9.8 %reshape.44 = f32[8,2,8,2,64,2]{5,4,3,2,1,0:T(8,128)} reshape(f32[16,16,128]{2,1,0:T(8,128)S(1)} %fusion.16) | data formatting | bytes 262144 | tf_op jit(solution)/shard_map/reshape | solution.py:59
  273.4 4.0 reduce_sum.48
  280.2 4.0 broadcast_in_dim.11
  284.1 6.9 %reshape.47 = f32[16,16,128]{2,1,0:T(8,128)S(1)} reshape(f32[8,2,8,2,64,2]{5,4,3,2,1,0:T(8,128)} %broadcast_in_dim.11) | data formatting | bytes 262144 | tf_op jit(solution)/shard_map/reshape | solution.py:68
  302.2 4.2 collective-permute-done.45
  309.1 3.2 collective-permute-start.47
  312.3 3.7 collective-permute-done.47
  327.5 4.2 collective-permute-done.51
  333.7 3.9 collective-permute-start.53
  348.5 3.9 collective-permute-start.56
  353.7 4.2 collective-permute-done.57
  360.0 3.9 collective-permute-start.59
  374.5 3.9 collective-permute-start.62
  379.8 4.2 collective-permute-done.63
  386.0 3.9 collective-permute-start.65
  393.7 4.0 broadcast_in_dim.14
  397.6 6.9 %reshape.50 = f32[16,16,128]{2,1,0:T(8,128)S(1)} reshape(f32[8,2,8,2,64,2]{5,4,3,2,1,0:T(8,128)} %broadcast_in_dim.14) | data formatting | bytes 262144 | tf_op jit(solution)/shard_map/reshape | solution.py:68
  416.0 4.2 collective-permute-done.69
  422.3 3.9 collective-permute-start.71
  443.0 4.2 collective-permute-done.75
  449.2 3.9 collective-permute-start.77
  469.9 4.2 collective-permute-done.81
  476.2 3.9 collective-permute-start.83
  (247 shorter events, 229.4 us)
Async XLA Ops:
  1.3 5.6 %collective-permute-start.1 = (f32[1,16,128]{2,1,0:T(8,128)S(1)}, f32[1,16,128]{2,1,0:T(8,128)S(1)}, u32[]{:S(2)}, u32[]{:S(2)}) collective-permute-start(f32[1,16,128]{2,1,0:T(8,128)S(1)} %get-tuple-element.56), channel_id=1, source_target_pairs={{0,1},{1,2},{2,3},{3,4},{4,5},{5,6},{6,7},{8,9},{9,10},{10,11},{11... | collective-permute-start | bytes 24584 | tf_op jit(solution)/shard_map/ppermute | solution.py:22
  3.3 5.0 %collective-permute-start = (f32[1,16,128]{2,1,0:T(8,128)S(1)}, f32[1,16,128]{2,1,0:T(8,128)S(1)}, u32[]{:S(2)}, u32[]{:S(2)}) collective-permute-start(f32[1,16,128]{2,1,0:T(8,128)S(1)} %get-tuple-element.55), channel_id=1, source_target_pairs={{1,0},{2,1},{3,2},{4,3},{5,4},{6,5},{7,6},{9,8},{10,9},{11,10},{12... | collective-permute-start | bytes 24584 | tf_op jit(solution)/shard_map/ppermute | solution.py:23
  11.5 5.6 %collective-permute-start.3 = (f32[18,1,128]{2,1,0:T(1,128)S(1)}, f32[18,1,128]{2,1,0:T(1,128)S(1)}, u32[]{:S(2)}, u32[]{:S(2)}) collective-permute-start(f32[18,1,128]{2,1,0:T(1,128)S(1)} %get-tuple-element.39), channel_id=1, source_target_pairs={{0,64},{64,128},{128,192},{192,256},{256,320},{320,384},{384,448},... | collective-permute-start | bytes 27656 | tf_op jit(solution)/shard_map/ppermute | solution.py:22
  17.3 9.4 %collective-permute-start.4 = (f32[18,18,1]{2,1,0:T(8,128)S(1)}, f32[18,18,1]{2,1,0:T(8,128)S(1)}, u32[]{:S(2)}, u32[]{:S(2)}) collective-permute-start(f32[18,18,1]{2,1,0:T(8,128)S(1)} %get-tuple-element.27), channel_id=1, source_target_pairs={{8,0},{16,8},{24,16},{32,24},{40,32},{48,40},{56,48},{9,1},{17,9},... | collective-permute-start | bytes 3896 | tf_op jit(solution)/shard_map/ppermute | solution.py:23
  19.2 10.6 %collective-permute-start.5 = (f32[18,18,1]{2,1,0:T(8,128)S(1)}, f32[18,18,1]{2,1,0:T(8,128)S(1)}, u32[]{:S(2)}, u32[]{:S(2)}) collective-permute-start(f32[18,18,1]{2,1,0:T(8,128)S(1)} %get-tuple-element.28), channel_id=1, source_target_pairs={{0,8},{8,16},{16,24},{24,32},{32,40},{40,48},{48,56},{1,9},{9,17},... | collective-permute-start | bytes 3896 | tf_op jit(solution)/shard_map/ppermute | solution.py:22
  33.3 5.0 %collective-permute-start.7 = (f32[1,16,128]{2,1,0:T(8,128)S(1)}, f32[1,16,128]{2,1,0:T(8,128)S(1)}, u32[]{:S(2)}, u32[]{:S(2)}) collective-permute-start(f32[1,16,128]{2,1,0:T(8,128)S(1)} %get-tuple-element.53), channel_id=1, source_target_pairs={{0,1},{1,2},{2,3},{3,4},{4,5},{5,6},{6,7},{8,9},{9,10},{10,11},{11... | collective-permute-start | bytes 24584 | tf_op jit(solution)/shard_map/ppermute | solution.py:22
  41.5 5.6 %collective-permute-start.9 = (f32[18,1,128]{2,1,0:T(1,128)S(1)}, f32[18,1,128]{2,1,0:T(1,128)S(1)}, u32[]{:S(2)}, u32[]{:S(2)}) collective-permute-start(f32[18,1,128]{2,1,0:T(1,128)S(1)} %get-tuple-element.37), channel_id=1, source_target_pairs={{0,64},{64,128},{128,192},{192,256},{256,320},{320,384},{384,448},... | collective-permute-start | bytes 27656 | tf_op jit(solution)/shard_map/ppermute | solution.py:22
  47.2 7.8 %collective-permute-start.10 = (f32[18,18,1]{2,1,0:T(8,128)S(1)}, f32[18,18,1]{2,1,0:T(8,128)S(1)}, u32[]{:S(2)}, u32[]{:S(2)}) collective-permute-start(f32[18,18,1]{2,1,0:T(8,128)S(1)} %get-tuple-element.25), channel_id=1, source_target_pairs={{8,0},{16,8},{24,16},{32,24},{40,32},{48,40},{56,48},{9,1},{17,9},... | collective-permute-start | bytes 3896 | tf_op jit(solution)/shard_map/ppermute | solution.py:23
  49.2 9.0 %collective-permute-start.11 = (f32[18,18,1]{2,1,0:T(8,128)S(1)}, f32[18,18,1]{2,1,0:T(8,128)S(1)}, u32[]{:S(2)}, u32[]{:S(2)}) collective-permute-start(f32[18,18,1]{2,1,0:T(8,128)S(1)} %get-tuple-element.26), channel_id=1, source_target_pairs={{0,8},{8,16},{16,24},{24,32},{32,40},{40,48},{48,56},{1,9},{9,17},... | collective-permute-start | bytes 3896 | tf_op jit(solution)/shard_map/ppermute | solution.py:22
  61.3 5.0 %collective-permute-start.13 = (f32[1,16,128]{2,1,0:T(8,128)S(1)}, f32[1,16,128]{2,1,0:T(8,128)S(1)}, u32[]{:S(2)}, u32[]{:S(2)}) collective-permute-start(f32[1,16,128]{2,1,0:T(8,128)S(1)} %get-tuple-element.51), channel_id=1, source_target_pairs={{0,1},{1,2},{2,3},{3,4},{4,5},{5,6},{6,7},{8,9},{9,10},{10,11},{11... | collective-permute-start | bytes 24584 | tf_op jit(solution)/shard_map/ppermute | solution.py:22
  69.5 5.6 %collective-permute-start.15 = (f32[18,1,128]{2,1,0:T(1,128)S(1)}, f32[18,1,128]{2,1,0:T(1,128)S(1)}, u32[]{:S(2)}, u32[]{:S(2)}) collective-permute-start(f32[18,1,128]{2,1,0:T(1,128)S(1)} %get-tuple-element.35), channel_id=1, source_target_pairs={{0,64},{64,128},{128,192},{192,256},{256,320},{320,384},{384,448},... | collective-permute-start | bytes 27656 | tf_op jit(solution)/shard_map/ppermute | solution.py:22
  75.2 7.8 %collective-permute-start.16 = (f32[18,18,1]{2,1,0:T(8,128)S(1)}, f32[18,18,1]{2,1,0:T(8,128)S(1)}, u32[]{:S(2)}, u32[]{:S(2)}) collective-permute-start(f32[18,18,1]{2,1,0:T(8,128)S(1)} %get-tuple-element.23), channel_id=1, source_target_pairs={{8,0},{16,8},{24,16},{32,24},{40,32},{48,40},{56,48},{9,1},{17,9},... | collective-permute-start | bytes 3896 | tf_op jit(solution)/shard_map/ppermute | solution.py:23
  77.2 9.0 %collective-permute-start.17 = (f32[18,18,1]{2,1,0:T(8,128)S(1)}, f32[18,18,1]{2,1,0:T(8,128)S(1)}, u32[]{:S(2)}, u32[]{:S(2)}) collective-permute-start(f32[18,18,1]{2,1,0:T(8,128)S(1)} %get-tuple-element.24), channel_id=1, source_target_pairs={{0,8},{8,16},{16,24},{24,32},{32,40},{40,48},{48,56},{1,9},{9,17},... | collective-permute-start | bytes 3896 | tf_op jit(solution)/shard_map/ppermute | solution.py:22
  111.6 5.5 %collective-permute-start.21 = (f32[10,1,64]{2,1,0:T(1,128)S(1)}, f32[10,1,64]{2,1,0:T(1,128)S(1)}, u32[]{:S(2)}, u32[]{:S(2)}) collective-permute-start(f32[10,1,64]{2,1,0:T(1,128)S(1)} %get-tuple-element.71), channel_id=1, source_target_pairs={{0,64},{64,128},{128,192},{192,256},{256,320},{320,384},{384,448},... | collective-permute-start | bytes 7688 | tf_op jit(solution)/shard_map/ppermute | solution.py:22
  117.2 6.3 %collective-permute-start.22 = (f32[10,10,1]{2,1,0:T(8,128)S(1)}, f32[10,10,1]{2,1,0:T(8,128)S(1)}, u32[]{:S(2)}, u32[]{:S(2)}) collective-permute-start(f32[10,10,1]{2,1,0:T(8,128)S(1)} %get-tuple-element.63), channel_id=1, source_target_pairs={{8,0},{16,8},{24,16},{32,24},{40,32},{48,40},{56,48},{9,1},{17,9},... | collective-permute-start | bytes 1208 | tf_op jit(solution)/shard_map/ppermute | solution.py:23
  119.1 7.5 %collective-permute-start.23 = (f32[10,10,1]{2,1,0:T(8,128)S(1)}, f32[10,10,1]{2,1,0:T(8,128)S(1)}, u32[]{:S(2)}, u32[]{:S(2)}) collective-permute-start(f32[10,10,1]{2,1,0:T(8,128)S(1)} %get-tuple-element.64), channel_id=1, source_target_pairs={{0,8},{8,16},{16,24},{24,32},{32,40},{40,48},{48,56},{1,9},{9,17},... | collective-permute-start | bytes 1208 | tf_op jit(solution)/shard_map/ppermute | solution.py:22
  136.8 5.5 %collective-permute-start.27 = (f32[10,1,64]{2,1,0:T(1,128)S(1)}, f32[10,1,64]{2,1,0:T(1,128)S(1)}, u32[]{:S(2)}, u32[]{:S(2)}) collective-permute-start(f32[10,1,64]{2,1,0:T(1,128)S(1)} %get-tuple-element.69), channel_id=1, source_target_pairs={{0,64},{64,128},{128,192},{192,256},{256,320},{320,384},{384,448},... | collective-permute-start | bytes 7688 | tf_op jit(solution)/shard_map/ppermute | solution.py:22
  142.4 6.3 %collective-permute-start.28 = (f32[10,10,1]{2,1,0:T(8,128)S(1)}, f32[10,10,1]{2,1,0:T(8,128)S(1)}, u32[]{:S(2)}, u32[]{:S(2)}) collective-permute-start(f32[10,10,1]{2,1,0:T(8,128)S(1)} %get-tuple-element.61), channel_id=1, source_target_pairs={{8,0},{16,8},{24,16},{32,24},{40,32},{48,40},{56,48},{9,1},{17,9},... | collective-permute-start | bytes 1208 | tf_op jit(solution)/shard_map/ppermute | solution.py:23
  144.4 7.5 %collective-permute-start.29 = (f32[10,10,1]{2,1,0:T(8,128)S(1)}, f32[10,10,1]{2,1,0:T(8,128)S(1)}, u32[]{:S(2)}, u32[]{:S(2)}) collective-permute-start(f32[10,10,1]{2,1,0:T(8,128)S(1)} %get-tuple-element.62), channel_id=1, source_target_pairs={{0,8},{8,16},{16,24},{24,32},{32,40},{40,48},{48,56},{1,9},{9,17},... | collective-permute-start | bytes 1208 | tf_op jit(solution)/shard_map/ppermute | solution.py:22
  163.3 5.5 %collective-permute-start.33 = (f32[6,1,32]{2,1,0:T(1,128)S(1)}, f32[6,1,32]{2,1,0:T(1,128)S(1)}, u32[]{:S(2)}, u32[]{:S(2)}) collective-permute-start(f32[6,1,32]{2,1,0:T(1,128)S(1)} %get-tuple-element.95), channel_id=1, source_target_pairs={{0,64},{64,128},{128,192},{192,256},{256,320},{320,384},{384,448},... | collective-permute-start | bytes 2312 | tf_op jit(solution)/shard_map/ppermute | solution.py:22
  168.9 5.9 %collective-permute-start.34 = (f32[6,6,1]{2,1,0:T(8,128)S(1)}, f32[6,6,1]{2,1,0:T(8,128)S(1)}, u32[]{:S(2)}, u32[]{:S(2)}) collective-permute-start(f32[6,6,1]{2,1,0:T(8,128)S(1)} %get-tuple-element.87), channel_id=1, source_target_pairs={{8,0},{16,8},{24,16},{32,24},{40,32},{48,40},{56,48},{9,1},{17,9},... | collective-permute-start | bytes 440 | tf_op jit(solution)/shard_map/ppermute | solution.py:23
  170.8 6.9 %collective-permute-start.35 = (f32[6,6,1]{2,1,0:T(8,128)S(1)}, f32[6,6,1]{2,1,0:T(8,128)S(1)}, u32[]{:S(2)}, u32[]{:S(2)}) collective-permute-start(f32[6,6,1]{2,1,0:T(8,128)S(1)} %get-tuple-element.88), channel_id=1, source_target_pairs={{0,8},{8,16},{16,24},{24,32},{32,40},{40,48},{48,56},{1,9},{9,17},... | collective-permute-start | bytes 440 | tf_op jit(solution)/shard_map/ppermute | solution.py:22
  187.8 5.5 %collective-permute-start.39 = (f32[6,1,32]{2,1,0:T(1,128)S(1)}, f32[6,1,32]{2,1,0:T(1,128)S(1)}, u32[]{:S(2)}, u32[]{:S(2)}) collective-permute-start(f32[6,1,32]{2,1,0:T(1,128)S(1)} %get-tuple-element.93), channel_id=1, source_target_pairs={{0,64},{64,128},{128,192},{192,256},{256,320},{320,384},{384,448},... | collective-permute-start | bytes 2312 | tf_op jit(solution)/shard_map/ppermute | solution.py:22
  193.4 5.9 %collective-permute-start.40 = (f32[6,6,1]{2,1,0:T(8,128)S(1)}, f32[6,6,1]{2,1,0:T(8,128)S(1)}, u32[]{:S(2)}, u32[]{:S(2)}) collective-permute-start(f32[6,6,1]{2,1,0:T(8,128)S(1)} %get-tuple-element.85), channel_id=1, source_target_pairs={{8,0},{16,8},{24,16},{32,24},{40,32},{48,40},{56,48},{9,1},{17,9},... | collective-permute-start | bytes 440 | tf_op jit(solution)/shard_map/ppermute | solution.py:23
  195.3 6.9 %collective-permute-start.41 = (f32[6,6,1]{2,1,0:T(8,128)S(1)}, f32[6,6,1]{2,1,0:T(8,128)S(1)}, u32[]{:S(2)}, u32[]{:S(2)}) collective-permute-start(f32[6,6,1]{2,1,0:T(8,128)S(1)} %get-tuple-element.86), channel_id=1, source_target_pairs={{0,8},{8,16},{16,24},{24,32},{32,40},{40,48},{48,56},{1,9},{9,17},... | collective-permute-start | bytes 440 | tf_op jit(solution)/shard_map/ppermute | solution.py:22
  300.9 5.5 %collective-permute-start.45 = (f32[6,1,32]{2,1,0:T(1,128)S(1)}, f32[6,1,32]{2,1,0:T(1,128)S(1)}, u32[]{:S(2)}, u32[]{:S(2)}) collective-permute-start(f32[6,1,32]{2,1,0:T(1,128)S(1)} %get-tuple-element.91), channel_id=1, source_target_pairs={{0,64},{64,128},{128,192},{192,256},{256,320},{320,384},{384,448},... | collective-permute-start | bytes 2312 | tf_op jit(solution)/shard_map/ppermute | solution.py:22
  306.5 5.9 %collective-permute-start.46 = (f32[6,6,1]{2,1,0:T(8,128)S(1)}, f32[6,6,1]{2,1,0:T(8,128)S(1)}, u32[]{:S(2)}, u32[]{:S(2)}) collective-permute-start(f32[6,6,1]{2,1,0:T(8,128)S(1)} %get-tuple-element.83), channel_id=1, source_target_pairs={{8,0},{16,8},{24,16},{32,24},{40,32},{48,40},{56,48},{9,1},{17,9},... | collective-permute-start | bytes 440 | tf_op jit(solution)/shard_map/ppermute | solution.py:23
  309.1 6.9 %collective-permute-start.47 = (f32[6,6,1]{2,1,0:T(8,128)S(1)}, f32[6,6,1]{2,1,0:T(8,128)S(1)}, u32[]{:S(2)}, u32[]{:S(2)}) collective-permute-start(f32[6,6,1]{2,1,0:T(8,128)S(1)} %get-tuple-element.84), channel_id=1, source_target_pairs={{0,8},{8,16},{16,24},{24,32},{32,40},{40,48},{48,56},{1,9},{9,17},... | collective-permute-start | bytes 440 | tf_op jit(solution)/shard_map/ppermute | solution.py:22
  326.2 5.5 %collective-permute-start.51 = (f32[6,1,32]{2,1,0:T(1,128)S(1)}, f32[6,1,32]{2,1,0:T(1,128)S(1)}, u32[]{:S(2)}, u32[]{:S(2)}) collective-permute-start(f32[6,1,32]{2,1,0:T(1,128)S(1)} %get-tuple-element.89), channel_id=1, source_target_pairs={{0,64},{64,128},{128,192},{192,256},{256,320},{320,384},{384,448},... | collective-permute-start | bytes 2312 | tf_op jit(solution)/shard_map/ppermute | solution.py:22
  331.7 5.9 %collective-permute-start.52 = (f32[6,6,1]{2,1,0:T(8,128)S(1)}, f32[6,6,1]{2,1,0:T(8,128)S(1)}, u32[]{:S(2)}, u32[]{:S(2)}) collective-permute-start(f32[6,6,1]{2,1,0:T(8,128)S(1)} %get-tuple-element.81), channel_id=1, source_target_pairs={{8,0},{16,8},{24,16},{32,24},{40,32},{48,40},{56,48},{9,1},{17,9},... | collective-permute-start | bytes 440 | tf_op jit(solution)/shard_map/ppermute | solution.py:23
  333.7 6.9 %collective-permute-start.53 = (f32[6,6,1]{2,1,0:T(8,128)S(1)}, f32[6,6,1]{2,1,0:T(8,128)S(1)}, u32[]{:S(2)}, u32[]{:S(2)}) collective-permute-start(f32[6,6,1]{2,1,0:T(8,128)S(1)} %get-tuple-element.82), channel_id=1, source_target_pairs={{0,8},{8,16},{16,24},{24,32},{32,40},{40,48},{48,56},{1,9},{9,17},... | collective-permute-start | bytes 440 | tf_op jit(solution)/shard_map/ppermute | solution.py:22
  348.5 5.2 %collective-permute-start.56 = (f32[10,1,64]{2,1,0:T(1,128)S(1)}, f32[10,1,64]{2,1,0:T(1,128)S(1)}, u32[]{:S(2)}, u32[]{:S(2)}) collective-permute-start(f32[10,1,64]{2,1,0:T(1,128)S(1)} %get-tuple-element.68), channel_id=1, source_target_pairs={{64,0},{128,64},{192,128},{256,192},{320,256},{384,320},{448,384},... | collective-permute-start | bytes 7688 | tf_op jit(solution)/shard_map/ppermute | solution.py:23
  352.4 5.5 %collective-permute-start.57 = (f32[10,1,64]{2,1,0:T(1,128)S(1)}, f32[10,1,64]{2,1,0:T(1,128)S(1)}, u32[]{:S(2)}, u32[]{:S(2)}) collective-permute-start(f32[10,1,64]{2,1,0:T(1,128)S(1)} %get-tuple-element.67), channel_id=1, source_target_pairs={{0,64},{64,128},{128,192},{192,256},{256,320},{320,384},{384,448},... | collective-permute-start | bytes 7688 | tf_op jit(solution)/shard_map/ppermute | solution.py:22
  358.0 6.3 %collective-permute-start.58 = (f32[10,10,1]{2,1,0:T(8,128)S(1)}, f32[10,10,1]{2,1,0:T(8,128)S(1)}, u32[]{:S(2)}, u32[]{:S(2)}) collective-permute-start(f32[10,10,1]{2,1,0:T(8,128)S(1)} %get-tuple-element.59), channel_id=1, source_target_pairs={{8,0},{16,8},{24,16},{32,24},{40,32},{48,40},{56,48},{9,1},{17,9},... | collective-permute-start | bytes 1208 | tf_op jit(solution)/shard_map/ppermute | solution.py:23
  360.0 7.5 %collective-permute-start.59 = (f32[10,10,1]{2,1,0:T(8,128)S(1)}, f32[10,10,1]{2,1,0:T(8,128)S(1)}, u32[]{:S(2)}, u32[]{:S(2)}) collective-permute-start(f32[10,10,1]{2,1,0:T(8,128)S(1)} %get-tuple-element.60), channel_id=1, source_target_pairs={{0,8},{8,16},{16,24},{24,32},{32,40},{40,48},{48,56},{1,9},{9,17},... | collective-permute-start | bytes 1208 | tf_op jit(solution)/shard_map/ppermute | solution.py:22
  374.5 5.2 %collective-permute-start.62 = (f32[10,1,64]{2,1,0:T(1,128)S(1)}, f32[10,1,64]{2,1,0:T(1,128)S(1)}, u32[]{:S(2)}, u32[]{:S(2)}) collective-permute-start(f32[10,1,64]{2,1,0:T(1,128)S(1)} %get-tuple-element.66), channel_id=1, source_target_pairs={{64,0},{128,64},{192,128},{256,192},{320,256},{384,320},{448,384},... | collective-permute-start | bytes 7688 | tf_op jit(solution)/shard_map/ppermute | solution.py:23
  378.4 5.5 %collective-permute-start.63 = (f32[10,1,64]{2,1,0:T(1,128)S(1)}, f32[10,1,64]{2,1,0:T(1,128)S(1)}, u32[]{:S(2)}, u32[]{:S(2)}) collective-permute-start(f32[10,1,64]{2,1,0:T(1,128)S(1)} %get-tuple-element.65), channel_id=1, source_target_pairs={{0,64},{64,128},{128,192},{192,256},{256,320},{320,384},{384,448},... | collective-permute-start | bytes 7688 | tf_op jit(solution)/shard_map/ppermute | solution.py:22
  384.1 6.3 %collective-permute-start.64 = (f32[10,10,1]{2,1,0:T(8,128)S(1)}, f32[10,10,1]{2,1,0:T(8,128)S(1)}, u32[]{:S(2)}, u32[]{:S(2)}) collective-permute-start(f32[10,10,1]{2,1,0:T(8,128)S(1)} %get-tuple-element.57), channel_id=1, source_target_pairs={{8,0},{16,8},{24,16},{32,24},{40,32},{48,40},{56,48},{9,1},{17,9},... | collective-permute-start | bytes 1208 | tf_op jit(solution)/shard_map/ppermute | solution.py:23
  386.0 7.5 %collective-permute-start.65 = (f32[10,10,1]{2,1,0:T(8,128)S(1)}, f32[10,10,1]{2,1,0:T(8,128)S(1)}, u32[]{:S(2)}, u32[]{:S(2)}) collective-permute-start(f32[10,10,1]{2,1,0:T(8,128)S(1)} %get-tuple-element.58), channel_id=1, source_target_pairs={{0,8},{8,16},{16,24},{24,32},{32,40},{40,48},{48,56},{1,9},{9,17},... | collective-permute-start | bytes 1208 | tf_op jit(solution)/shard_map/ppermute | solution.py:22
  414.6 5.6 %collective-permute-start.69 = (f32[18,1,128]{2,1,0:T(1,128)S(1)}, f32[18,1,128]{2,1,0:T(1,128)S(1)}, u32[]{:S(2)}, u32[]{:S(2)}) collective-permute-start(f32[18,1,128]{2,1,0:T(1,128)S(1)} %get-tuple-element.33), channel_id=1, source_target_pairs={{0,64},{64,128},{128,192},{192,256},{256,320},{320,384},{384,448},... | collective-permute-start | bytes 27656 | tf_op jit(solution)/shard_map/ppermute | solution.py:22
  420.3 7.8 %collective-permute-start.70 = (f32[18,18,1]{2,1,0:T(8,128)S(1)}, f32[18,18,1]{2,1,0:T(8,128)S(1)}, u32[]{:S(2)}, u32[]{:S(2)}) collective-permute-start(f32[18,18,1]{2,1,0:T(8,128)S(1)} %get-tuple-element.21), channel_id=1, source_target_pairs={{8,0},{16,8},{24,16},{32,24},{40,32},{48,40},{56,48},{9,1},{17,9},... | collective-permute-start | bytes 3896 | tf_op jit(solution)/shard_map/ppermute | solution.py:23
  422.3 9.0 %collective-permute-start.71 = (f32[18,18,1]{2,1,0:T(8,128)S(1)}, f32[18,18,1]{2,1,0:T(8,128)S(1)}, u32[]{:S(2)}, u32[]{:S(2)}) collective-permute-start(f32[18,18,1]{2,1,0:T(8,128)S(1)} %get-tuple-element.22), channel_id=1, source_target_pairs={{0,8},{8,16},{16,24},{24,32},{32,40},{40,48},{48,56},{1,9},{9,17},... | collective-permute-start | bytes 3896 | tf_op jit(solution)/shard_map/ppermute | solution.py:22
  441.6 5.6 %collective-permute-start.75 = (f32[18,1,128]{2,1,0:T(1,128)S(1)}, f32[18,1,128]{2,1,0:T(1,128)S(1)}, u32[]{:S(2)}, u32[]{:S(2)}) collective-permute-start(f32[18,1,128]{2,1,0:T(1,128)S(1)} %get-tuple-element.31), channel_id=1, source_target_pairs={{0,64},{64,128},{128,192},{192,256},{256,320},{320,384},{384,448},... | collective-permute-start | bytes 27656 | tf_op jit(solution)/shard_map/ppermute | solution.py:22
  447.3 7.8 %collective-permute-start.76 = (f32[18,18,1]{2,1,0:T(8,128)S(1)}, f32[18,18,1]{2,1,0:T(8,128)S(1)}, u32[]{:S(2)}, u32[]{:S(2)}) collective-permute-start(f32[18,18,1]{2,1,0:T(8,128)S(1)} %get-tuple-element.19), channel_id=1, source_target_pairs={{8,0},{16,8},{24,16},{32,24},{40,32},{48,40},{56,48},{9,1},{17,9},... | collective-permute-start | bytes 3896 | tf_op jit(solution)/shard_map/ppermute | solution.py:23
  449.2 9.0 %collective-permute-start.77 = (f32[18,18,1]{2,1,0:T(8,128)S(1)}, f32[18,18,1]{2,1,0:T(8,128)S(1)}, u32[]{:S(2)}, u32[]{:S(2)}) collective-permute-start(f32[18,18,1]{2,1,0:T(8,128)S(1)} %get-tuple-element.20), channel_id=1, source_target_pairs={{0,8},{8,16},{16,24},{24,32},{32,40},{40,48},{48,56},{1,9},{9,17},... | collective-permute-start | bytes 3896 | tf_op jit(solution)/shard_map/ppermute | solution.py:22
  468.6 5.6 %collective-permute-start.81 = (f32[18,1,128]{2,1,0:T(1,128)S(1)}, f32[18,1,128]{2,1,0:T(1,128)S(1)}, u32[]{:S(2)}, u32[]{:S(2)}) collective-permute-start(f32[18,1,128]{2,1,0:T(1,128)S(1)} %get-tuple-element.29), channel_id=1, source_target_pairs={{0,64},{64,128},{128,192},{192,256},{256,320},{320,384},{384,448},... | collective-permute-start | bytes 27656 | tf_op jit(solution)/shard_map/ppermute | solution.py:22
  474.3 7.8 %collective-permute-start.82 = (f32[18,18,1]{2,1,0:T(8,128)S(1)}, f32[18,18,1]{2,1,0:T(8,128)S(1)}, u32[]{:S(2)}, u32[]{:S(2)}) collective-permute-start(f32[18,18,1]{2,1,0:T(8,128)S(1)} %get-tuple-element.17), channel_id=1, source_target_pairs={{8,0},{16,8},{24,16},{32,24},{40,32},{48,40},{56,48},{9,1},{17,9},... | collective-permute-start | bytes 3896 | tf_op jit(solution)/shard_map/ppermute | solution.py:23
  476.2 9.0 %collective-permute-start.83 = (f32[18,18,1]{2,1,0:T(8,128)S(1)}, f32[18,18,1]{2,1,0:T(8,128)S(1)}, u32[]{:S(2)}, u32[]{:S(2)}) collective-permute-start(f32[18,18,1]{2,1,0:T(8,128)S(1)} %get-tuple-element.18), channel_id=1, source_target_pairs={{0,8},{8,16},{16,24},{24,32},{32,40},{40,48},{48,56},{1,9},{9,17},... | collective-permute-start | bytes 3896 | tf_op jit(solution)/shard_map/ppermute | solution.py:22
  (39 other events, 241.6 us)
where the time goes:
time: 489 us; the launch traced here: 486 us
  starting transfers between devices  207 us (42%)
  waiting for transfers between devices  152 us (31%)
  blocking collectives  60.5 us (12%)
  local copies, waits for them, and re-layouts  48.5 us (10%)
  other arithmetic  16.1 us (3%)
    ppermute x42, waiting for transfers between devices, extended(): before = lax.ppermute(last, axis, up)  136 us
    ppermute x42, starting transfers between devices, extended(): before = lax.ppermute(last, axis, up)  105 us
    ppermute x42, starting transfers between devices, extended(): after = lax.ppermute(first, axis, down)  102 us
    all_gather x1, blocking collectives, collect(): return lax.all_gather(gathered, 'gx', axis=1, tiled=True)  24.8 us
    all_gather x1, blocking collectives, collect(): gathered = lax.all_gather(gathered, 'gy', axis=2, tiled=True)  24.6 us
    reshape x5, local copies, waits for them, and re-layouts, restrict(): blocks = values.reshape(shape_a // 2, 2, shape_b // 2, 2, shape_c // 2, 2)  21.8 us
    ppermute x42, waiting for transfers between devices, extended(): after = lax.ppermute(first, axis, down)  16.1 us
    reshape x5, local copies, waits for them, and re-layouts, prolong(): return spread.reshape(2 * shape_a, 2 * shape_b, 2 * shape_c)  15.2 us
  transfers between devices with their start and end apart: 84, of which 58 were waited for; matrix products, arithmetic and copies ran while one was open for 0% of the time, Pallas kernels for 0%

commit v1 on v0

v1 whole, which is shorter than its diff:
```python
import functools

import jax
import jax.numpy as jnp
from jax import lax
from jax.experimental import pallas as pl
from jax.experimental.pallas import tpu as pltpu
from jax.sharding import PartitionSpec as P

FIRST = 1.0 / 7.5
RHO = 1.0 / (2.0 * (5.0 / 3.0) - 0.6)
CARRY = 0.6 * RHO
FRESH = 2.0 * RHO / (0.75 * 6.0)
ALPHA = FIRST * (1.0 + CARRY) + FRESH
BETA = FRESH * FIRST
OWN = ALPHA - 6.0 * BETA

LANES = 128
RING = 8

SHIFTS = {
    "x0+": ("gx", 1, 32, 8), "x0-": ("gx", -1, 32, 8),
    "x1+": ("gx", 1, 12, 8), "x1-": ("gx", -1, 12, 8),
    "x2+1": ("gx", 1, 8, 8), "x2-1": ("gx", -1, 8, 8),
    "x2+2": ("gx", 2, 8, 8), "x2-2": ("gx", -2, 8, 8),
    "z0+": ("gz", 1, 9, 32), "z0-": ("gz", -1, 9, 32),
    "z1+": ("gz", 1, 7, 24), "z1-": ("gz", -1, 7, 24),
    "z2+1": ("gz", 1, 7, 16), "z2-1": ("gz", -1, 7, 16),
    "z2+2": ("gz", 2, 3, 16), "z2-2": ("gz", -2, 3, 16),
    "y0+": ("gy", 1, 4, 32), "y0-": ("gy", -1, 4, 32),
    "y1+": ("gy", 1, 2, 24), "y1-": ("gy", -1, 2, 24),
    "y2+": ("gy", 1, 1, 16), "y2-": ("gy", -1, 1, 16),
    "y3+": ("gy", 1, 4, 16), "y3-": ("gy", -1, 4, 16),
}
GATHERS = {"gx3": ("gx", 8), "gz3": ("gz", 16), "gy4": ("gy", 8)}


def iota(shape, dim):
    return lax.broadcasted_iota(jnp.int32, shape, dim)


def number(cond):
    return jnp.where(cond, 1.0, 0.0).astype(jnp.float32)


def dot(a, b):
    return jnp.dot(a, b, precision=lax.Precision.HIGHEST, preferred_element_type=jnp.float32)


def select_matrix(shape, hit, value=1.0):
    return number(hit(iota(shape, 0), iota(shape, 1))) * value


def rows_of(stacked, rows):
    return [stacked[i * rows:(i + 1) * rows] for i in range(stacked.shape[0] // rows)]


def lanes_of(stacked):
    return [stacked[:, i * LANES:(i + 1) * LANES] for i in range(stacked.shape[1] // LANES)]


def right(planes, matrix):
    return rows_of(dot(jnp.concatenate(planes, axis=0), matrix), planes[0].shape[0])


def left(matrix, planes):
    return lanes_of(dot(matrix, jnp.concatenate(planes, axis=1)))


def total(terms):
    terms = [t for t in terms if t is not None]
    out = terms[0]
    for t in terms[1:]:
        out = out + t
    return out


class Field:
    def __init__(self, lo, hi, make):
        self.lo, self.hi, self.make, self.have = lo, hi, make, {}

    def __call__(self, z):
        if z < self.lo or z > self.hi:
            return None
        if z not in self.have:
            self.have[z] = self.make(z)
        return self.have[z]


def field_of(lo, planes):
    return Field(lo, lo + len(planes) - 1, lambda z: planes[z - lo])


class Math:
    def __init__(self, env):
        self.env = env
        self.iz, self.ix, self.iy = env.position

    def roll(self, v, shift, axis):
        shift = shift % v.shape[axis]
        return v if shift == 0 else self.env.roll(v, shift, axis)

    def place_rows(self, v, at, rows):
        pad = jnp.zeros((rows - v.shape[0],) + v.shape[1:], v.dtype)
        return self.roll(jnp.concatenate([v, pad], axis=0), at, 0)

    def take_rows(self, v, at, rows):
        return self.roll(v, -at, 0)[:rows]

    def mask(self, level, rows, row_off, lanes, own_y):
        nz, nx, ny = 16 >> level, 16 >> level, 128 >> level
        x = iota((rows, lanes), 0) - row_off + self.ix * nx
        lane = iota((rows, lanes), 1)
        y = jnp.where(lane < (own_y + lanes) // 2, lane, lane - lanes) + self.iy * ny
        flat = number((x >= 0) & (x < 128 >> level) & (y >= 0) & (y < 1024 >> level))

        def make(z):
            if 0 <= z < nz:
                return flat
            at = self.iz * nz + z
            return flat * number((at >= 0) & (at < 128 >> level))

        return Field(-16, 32, make)

    def beside(self, f, z):
        v = f(z)
        terms = [f(z - 1), f(z + 1)]
        if v is not None:
            terms += [self.roll(v, 1, 0), self.roll(v, -1, 0), self.roll(v, 1, 1), self.roll(v, -1, 1)]
        return total(terms)

    def correction(self, r, mask, lo, hi):
        def make(z):
            v = r(z)
            near = BETA * self.beside(r, z)
            return mask(z) * (near if v is None else OWN * v + near)
        return Field(lo, hi, make)

    def minus_op(self, b, x, mask, lo, hi):
        def make(z):
            out = self.beside(x, z)
            if x(z) is not None:
                out = out - 6.0 * x(z)
            if b(z) is not None:
                out = out + b(z)
            return mask(z) * out
        return Field(lo, hi, make)

    def slots(self, rows, start):
        lane = (iota((rows, LANES), 1) - start) % LANES
        return number(lane < 8)

    def pack(self, planes, start):
        rows = planes[0].shape[0]
        tiles = []
        for g in range(0, len(planes), 16):
            tile = None
            for w, plane in enumerate(planes[g:g + 16]):
                part = self.slots(rows, 8 * w) * self.roll(plane, 8 * w - start, 1)
                tile = part if tile is None else tile + part
            tiles.append(tile)
        return tiles

    def unpack(self, tiles, count, start):
        keep = self.slots(tiles[0].shape[0], start)
        return [keep * self.roll(tiles[i // 16], start - 8 * (i % 16), 1) for i in range(count)]


def cycle(env, x_own, b_own):
    m = Math(env)
    iz, ix, iy = env.position
    zeros = lambda *s: jnp.zeros(s, jnp.float32)

    mask0 = m.mask(0, 24, 4, 256, 128)
    put0 = lambda v: jnp.concatenate([m.place_rows(v, 4, 24), zeros(24, LANES)], axis=1)
    xc = Field(0, 15, lambda z: put0(x_own[z]))
    bc = Field(0, 15, lambda z: put0(b_own[z]))
    r0 = m.minus_op(bc, xc, mask0, -1, 16)
    u0 = m.correction(r0, mask0, -2, 17)
    p0 = m.minus_op(r0, u0, mask0, -3, 18)
    coarse = [total([p0(2 * z), p0(2 * z + 1)]) for z in range(-2, 10)]
    coarse = right(coarse, select_matrix((256, 128), lambda a, c: (a >> 1) == c, 0.5))
    coarse = left(select_matrix((16, 24), lambda a, c: (c >> 1) + 2 == a), coarse)
    mask1c = m.mask(1, 16, 4, 128, 64)
    b1c = field_of(-2, [mask1c(z) * v for z, v in zip(range(-2, 10), coarse)])

    u1 = m.correction(b1c, mask1c, -3, 10)
    p1 = m.minus_op(b1c, u1, mask1c, -4, 11)
    coarse = [total([p1(2 * z), p1(2 * z + 1)]) for z in range(-2, 6)]
    half = select_matrix((128, 128), lambda a, c: (a >> 1) + jnp.where(a >= 96, 64, 0) == c, 0.5)
    coarse = right(coarse, half)
    halve_rows = select_matrix((8, 16), lambda a, c: (c >> 1) == a)
    coarse = left(halve_rows, coarse)
    mask2e = m.mask(2, 8, 2, 128, 32)
    b2c = [mask2e(z) * v for z, v in zip(range(-2, 6), coarse)]

    mask2c = m.mask(2, 16, 4, 128, 32)
    b2p = field_of(-2, [m.place_rows(v, 2, 16) for v in b2c])
    u2 = m.correction(b2p, mask2c, -3, 6)
    p2 = m.minus_op(b2p, u2, mask2c, -4, 7)
    coarse = [total([p2(2 * z), p2(2 * z + 1)]) for z in range(-2, 4)]
    half = select_matrix((128, 128), lambda a, c: (jnp.where(a < 80, a, a - 128) >> 1) + 2 == c, 0.5)
    coarse = left(halve_rows, right(coarse, half))
    b3c = total([m.roll(v, 20 * s, 1) for s, v in enumerate(coarse)])

    env.ready()
    env.gather_send("gx3", b3c)
    for d in (1, -1, 2, -2):
        env.shift_send("x2%+d" % d, b2c)
    env.shift_send("x1+", [m.take_rows(b1c(z), 7, 8) for z in range(-2, 10)])
    env.shift_send("x1-", [m.take_rows(b1c(z), 2, 8) for z in range(-2, 10)])
    env.shift_send("x0+", [v[8:] for v in x_own] + [v[8:] for v in b_own])
    env.shift_send("x0-", [v[:8] for v in x_own] + [v[:8] for v in b_own])

    parts = env.gather_recv("gx3")
    wide = total([m.place_rows(v, 2 * k, 24) for k, v in enumerate(parts)])
    b3x = m.take_rows(wide, 2, 16)

    env.gather_send("gz3", b3x)

    got = {d: env.shift_recv("x2%+d" % d) for d in (1, -1, 2, -2)}
    row8 = iota((8, LANES), 0)
    low, high = number(row8 < 4), number(row8 >= 4)
    b2x = []
    for i in range(8):
        lo = got[1][i] + low * m.roll(got[2][i], 4, 0)
        hi = got[-1][i] + high * m.roll(got[-2][i], 4, 0)
        b2x.append(jnp.concatenate([lo, hi], axis=0) + m.place_rows(b2c[i], 4, 16))
    env.shift_send("z2+1", b2x[1:])
    env.shift_send("z2-1", b2x[:7])
    env.shift_send("z2+2", b2x[5:])
    env.shift_send("z2-2", b2x[:3])

    before, after = env.shift_recv("x1+"), env.shift_recv("x1-")
    b1x = [
        m.place_rows(b1c(i - 2), 4, 24) + m.place_rows(before[i], 3, 24) + m.place_rows(after[i], 14, 24)
        for i in range(12)
    ]
    env.shift_send("z1+", b1x[5:])
    env.shift_send("z1-", b1x[:7])

    before, after = env.shift_recv("x0+"), env.shift_recv("x0-")
    own = x_own + b_own
    joined = [jnp.concatenate([before[i], own[i], after[i]], axis=0) for i in range(32)]
    x0x, b0x = joined[:16], joined[16:]
    env.shift_send("z0+", x0x[11:] + b0x[12:])
    env.shift_send("z0-", x0x[:5] + b0x[:4])

    parts = env.gather_recv("gz3")
    lane = iota((16, LANES), 1)
    tiles = []
    for q in range(4):
        tile = None
        for w in range(4):
            z = 4 * q + w
            here = []
            for k in range(RING):
                s = z - 2 * k + 2
                if 0 <= s < 6:
                    here.append(m.roll(parts[k], 32 * w + 6 - 20 * s, 1))
            at = lane - (32 * w + 6)
            part = number((at >= 0) & (at < 20)) * total(here)
            tile = part if tile is None else tile + part
        tiles.append(tile)
    row16, lane512 = iota((16, 512), 0), iota((16, 512), 1)
    slot = lane512 & 31
    y3 = slot - 8 + 16 * iy
    mask3 = number((y3 >= 0) & (y3 < 128))
    not_first, not_last = number(row16 > 0), number(row16 < 15)
    not_bottom, not_top = number(lane512 >= 32), number(lane512 < 480)

    def beside3(v):
        out = not_first * m.roll(v, 1, 0) + not_last * m.roll(v, -1, 0)
        out = out + not_bottom * m.roll(v, 32, 1) + not_top * m.roll(v, -32, 1)
        return out + m.roll(v, 1, 1) + m.roll(v, -1, 1)

    correction3 = lambda r: mask3 * (OWN * r + BETA * beside3(r))
    minus_op3 = lambda b, x: mask3 * (b - 6.0 * x + beside3(x))

    b3s = mask3 * jnp.concatenate(tiles, axis=1)
    p3 = minus_op3(b3s, correction3(b3s))
    gather_lanes = select_matrix((512, 128), lambda a, c: 16 * (a >> 6) + ((a & 31) >> 1) == c, 0.5)
    b4c = dot(halve_rows, dot(p3, gather_lanes))

    env.gather_send("gy4", b4c)
    env.shift_send("y3+", lanes_of(b3s))
    env.shift_send("y3-", lanes_of(b3s))

    got = {d: env.shift_recv("z2%+d" % d) for d in (1, -1, 2, -2)}
    b2w = []
    for z in range(-5, 9):
        here = []
        if -2 <= z <= 5:
            here.append(b2x[z + 2])
        if z <= 1:
            here.append(got[1][z + 5])
        if z >= 2:
            here.append(got[-1][z - 2])
        if z <= -3:
            here.append(got[2][z + 5])
        if z >= 6:
            here.append(got[-2][z - 6])
        b2w.append(total(here))
    env.shift_send("y2+", m.pack(b2w, 27))
    env.shift_send("y2-", m.pack(b2w, 126))

    before, after = env.shift_recv("z1+"), env.shift_recv("z1-")
    b1w = []
    for z in range(-5, 13):
        here = []
        if -2 <= z <= 9:
            here.append(b1x[z + 2])
        if z <= 1:
            here.append(before[z + 5])
        if z >= 6:
            here.append(after[z - 6])
        b1w.append(total(here))
    env.shift_send("y1+", m.pack(b1w, 59))
    env.shift_send("y1-", m.pack(b1w, 126))

    before, after = env.shift_recv("z0+"), env.shift_recv("z0-")
    x0w = before[:5] + x0x + after[:5]
    b0w = before[5:] + b0x + after[5:]
    env.shift_send("y0+", m.pack(x0w, 120) + m.pack(b0w, 120))
    env.shift_send("y0-", m.pack(x0w, 0) + m.pack(b0w, 0))

    parts = env.gather_recv("gy4")
    row, lane = iota((8, LANES), 0), iota((8, LANES), 1)
    keep = []
    for j in range(RING):
        at = lane - (8 * j - 4)
        keep.append(number((at >= 0) & (at < 16) & (lane < 64)))
    b4 = field_of(0, [
        total([keep[j] * m.roll(parts[j], 8 * j - 4 - 16 * z, 1) for j in range(RING)]) for z in range(8)
    ])
    mask4 = number(lane < 64)
    first8, last8 = number(row > 0), number(row < 7)

    def beside4(f, z):
        v = f(z)
        return total([
            f(z - 1), f(z + 1), first8 * m.roll(v, 1, 0), last8 * m.roll(v, -1, 0), m.roll(v, 1, 1), m.roll(v, -1, 1)
        ])

    def correction4(r):
        return Field(0, 7, lambda z: mask4 * (OWN * r(z) + BETA * beside4(r, z)))

    def minus_op4(b, x):
        return Field(0, 7, lambda z: mask4 * (b(z) - 6.0 * x(z) + beside4(x, z)))

    u4 = correction4(b4)
    p4 = minus_op4(b4, u4)
    half = select_matrix((128, 128), lambda a, c: ((a >> 1) == c) & (a < 64), 0.5)
    coarse = jnp.concatenate([p4(2 * z) + p4(2 * z + 1) for z in range(4)], axis=0)
    b5 = dot(select_matrix((16, 32), lambda a, c: (c >> 3) * 4 + ((c & 7) >> 1) == a), dot(coarse, half))

    row, lane = iota((16, LANES), 0), iota((16, LANES), 1)
    mask5 = number(lane < 32)
    first5, last5 = number((row & 3) > 0), number((row & 3) < 3)
    bottom5, top5 = number(row >= 4), number(row < 12)

    def beside5(v):
        out = first5 * m.roll(v, 1, 0) + last5 * m.roll(v, -1, 0)
        out = out + bottom5 * m.roll(v, 4, 0) + top5 * m.roll(v, -4, 0)
        return out + m.roll(v, 1, 1) + m.roll(v, -1, 1)

    u5 = mask5 * (OWN * b5 + BETA * beside5(b5))
    p5 = mask5 * (b5 - 6.0 * u5 + beside5(u5))
    e5 = u5 + mask5 * (OWN * p5 + BETA * beside5(p5))
    env.coarse_out(e5)

    double = select_matrix((128, 128), lambda a, c: (a == (c >> 1)) & (c < 64))
    wide = dot(select_matrix((32, 16), lambda a, c: (a >> 3) * 4 + ((a & 7) >> 1) == c), dot(e5, double))
    c4 = rows_of(wide, 8)
    c4 = field_of(0, [c4[z // 2] for z in range(8)])
    q4 = minus_op4(p4, c4)
    v4 = correction4(q4)
    e4 = [u4(z) + c4(z) + v4(z) for z in range(8)]

    own_y = select_matrix((128, 128), lambda a, c: (a == 8 * iy + (((c & 31) - 8) >> 1)) & (c < 64))
    planes = right(e4, own_y)
    wide = jnp.concatenate([planes[2 * k] + m.roll(planes[2 * k + 1], 64, 1) for k in range(4)], axis=1)
    c3 = mask3 * dot(select_matrix((16, 8), lambda a, c: (a >> 1) == c), wide)
    before = jnp.concatenate(env.shift_recv("y3+"), axis=1)
    after = jnp.concatenate(env.shift_recv("y3-"), axis=1)
    b3w = b3s + number((slot >= 3) & (slot < 10)) * m.roll(before, -16, 1)
    b3w = mask3 * (b3w + number((slot >= 22) & (slot < 29)) * m.roll(after, 16, 1))
    u3 = correction3(b3w)
    p3 = minus_op3(b3w, u3)
    e3 = u3 + c3 + correction3(minus_op3(p3, c3))

    spread = select_matrix((16, 16), lambda a, c: 2 * ix + ((a - 6) >> 1) == c)
    tiles = lanes_of(dot(spread, e3))
    near = env.window([m.roll(tiles[z // 4], -32 * (z % 4), 1) for z in range(16)])
    y_of = lambda c: jnp.where(c < 80, c, c - 128)
    own_y = select_matrix(
        (128, 128), lambda a, c: (a - 8 == (y_of(c) >> 1)) & (a < 32) & (y_of(c) < 36) & (y_of(c) >= -4))
    near = right(near, own_y)
    c2 = field_of(-4, [near[(z >> 1) + 2] for z in range(-4, 8)])

    def window(level, planes, tag, rows, row_off, lo, own_y, at_low, at_high):
        mask = m.mask(level, rows, row_off, LANES, own_y)
        before = m.unpack(env.shift_recv(tag + "+"), len(planes), at_low)
        after = m.unpack(env.shift_recv(tag + "-"), len(planes), at_high)
        return mask, field_of(lo, [
            mask(lo + i) * (v + before[i] + after[i]) for i, v in enumerate(planes)
        ])

    mask2, b2 = window(2, b2w, "y2", 16, 6, -5, 32, 123, 30)
    u2 = m.correction(b2, mask2, -4, 7)
    p2 = m.minus_op(b2, u2, mask2, -3, 6)
    v2 = m.correction(m.minus_op(p2, c2, mask2, -3, 6), mask2, -2, 5)
    e2 = [u2(z) + mask2(z) * c2(z) + v2(z) for z in range(-2, 6)]

    y_fine = lambda c: jnp.where(c < 96, c, c - 128)
    own_y = select_matrix((128, 128), lambda a, c: y_of(a) == (y_fine(c) >> 1))
    coarse = left(select_matrix((24, 16), lambda a, c: (a >> 1) + 2 == c), e2)
    coarse = right(coarse, own_y)
    c1 = field_of(-4, [coarse[(z >> 1) + 2] for z in range(-4, 12)])
    mask1, b1 = window(1, b1w, "y1", 24, 8, -5, 64, 123, 62)
    u1 = m.correction(b1, mask1, -4, 11)
    p1 = m.minus_op(b1, u1, mask1, -3, 10)
    v1 = m.correction(m.minus_op(p1, c1, mask1, -3, 10), mask1, -2, 9)
    e1 = [u1(z) + mask1(z) * c1(z) + v1(z) for z in range(-2, 10)]

    coarse = left(select_matrix((32, 24), lambda a, c: (a >> 1) + 4 == c), e1)
    coarse = right(coarse, select_matrix((128, 256), lambda a, c: a == (c >> 1)))
    c0 = field_of(-4, [coarse[(z >> 1) + 2] for z in range(-4, 20)])
    mask0 = m.mask(0, 32, 8, 256, 128)
    before, after = env.shift_recv("y0+"), env.shift_recv("y0-")

    def window0(planes, lo, some):
        low = m.unpack(before[some], len(planes), 120)
        high = m.unpack(after[some], len(planes), 0)
        return field_of(lo, [
            mask0(lo + i) * jnp.concatenate([v, low[i] + high[i]], axis=1) for i, v in enumerate(planes)
        ])

    x0 = window0(x0w, -5, slice(0, 2))
    b0 = window0(b0w, -4, slice(2, 4))
    r0 = m.minus_op(b0, x0, mask0, -4, 19)
    u0 = m.correction(r0, mask0, -3, 18)
    p0 = m.minus_op(r0, u0, mask0, -2, 17)
    q0 = m.minus_op(p0, c0, mask0, -2, 17)
    v0 = m.correction(q0, mask0, -1, 16)
    left_over = m.minus_op(q0, v0, mask0, 0, 15)
    inner = lambda v: v[8:24, :LANES]
    for z in range(16):
        env.fine_out(z, x_own[z] + inner(u0(z)) + inner(c0(z)) + inner(v0(z)), inner(left_over(z)))


class KernelEnv:
    def __init__(self, refs):
        self.refs = refs
        self.position = tuple(lax.axis_index(a) for a in ("gz", "gx", "gy"))
        self.at = dict(zip(("gz", "gx", "gy"), self.position))
        self.started = []
        self.barrier = pltpu.get_barrier_semaphore()
        for axis in ("gx", "gz", "gy"):
            for d in range(1, RING):
                pl.semaphore_signal(
                    self.barrier, inc=1, device_id={axis: self.peer(axis, d)}, device_id_type=pl.DeviceIdType.MESH)

    def peer(self, axis, d):
        return lax.rem(self.at[axis] + (d + RING), RING)

    def roll(self, v, shift, axis):
        return pltpu.roll(v, shift, axis)

    def ready(self):
        pl.semaphore_wait(self.barrier, 3 * (RING - 1))

    def copy(self, src, dst, send_sem, recv_sem, axis, d):
        return pltpu.make_async_remote_copy(
            src_ref=src, dst_ref=dst, send_sem=send_sem, recv_sem=recv_sem,
            device_id={axis: self.peer(axis, d)}, device_id_type=pl.DeviceIdType.MESH)

    def shift_copy(self, name):
        axis, d, _, _ = SHIFTS[name]
        i = list(SHIFTS).index(name)
        return self.copy(
            self.refs["out" + name], self.refs["in" + name], self.refs["shift_sems"].at[0, i],
            self.refs["shift_sems"].at[1, i], axis, d)

    def shift_send(self, name, planes):
        ref = self.refs["out" + name]
        for i, v in enumerate(planes):
            ref[i] = v
        copy = self.shift_copy(name)
        copy.start()
        self.started.append(copy)

    def shift_recv(self, name):
        self.shift_copy(name).wait_recv()
        ref = self.refs["in" + name]
        return [ref[i] for i in range(SHIFTS[name][2])]

    def gather_send(self, name, v):
        axis, _ = GATHERS[name]
        i = list(GATHERS).index(name)
        me = self.at[axis]
        buf, src, sems = self.refs["in" + name], self.refs["out" + name], self.refs["gather_sems"]
        src[...] = v
        for d in (1, 7, 2, 6, 3, 5, 4):
            copy = self.copy(src, buf.at[me], sems.at[0, i, d], sems.at[1, i, me], axis, d)
            copy.start()
            self.started.append(copy)
        buf[me] = v

    def gather_recv(self, name):
        axis, _ = GATHERS[name]
        i = list(GATHERS).index(name)
        buf, src, sems = self.refs["in" + name], self.refs["out" + name], self.refs["gather_sems"]
        for d in range(1, RING):
            k = self.peer(axis, d)
            self.copy(src, buf.at[k], sems.at[0, i, d], sems.at[1, i, k], axis, d).wait_recv()
        return [buf[k] for k in range(RING)]

    def window(self, planes):
        ref = self.refs["planes3"]
        zero = jnp.zeros((16, LANES), jnp.float32)
        for z in (0, 1, 18, 19):
            ref[z] = zero
        for z, v in enumerate(planes):
            ref[z + 2] = v
        return [ref[2 * self.position[0] + s] for s in range(6)]

    def coarse_out(self, v):
        for z in range(4):
            self.refs["coarse"][z] = v[4 * z:4 * z + 4, :32]

    def fine_out(self, z, pressure, residual):
        self.refs["pressure"][z] = pressure
        self.refs["residual"][z] = residual

    def finish(self):
        for copy in self.started:
            copy.wait_send()


def scratch():
    shapes = {}
    for name, (_, _, count, rows) in SHIFTS.items():
        shapes["out" + name] = pltpu.VMEM((count, rows, LANES), jnp.float32)
        shapes["in" + name] = pltpu.VMEM((count, rows, LANES), jnp.float32)
    for name, (_, rows) in GATHERS.items():
        shapes["out" + name] = pltpu.VMEM((rows, LANES), jnp.float32)
        shapes["in" + name] = pltpu.VMEM((RING, rows, LANES), jnp.float32)
    shapes["planes3"] = pltpu.VMEM((20, 16, LANES), jnp.float32)
    shapes["shift_sems"] = pltpu.SemaphoreType.DMA((2, len(SHIFTS)))
    shapes["gather_sems"] = pltpu.SemaphoreType.DMA((2, len(GATHERS), RING))
    return shapes


def kernel(names, divergence, previous, pressure, residual, coarse, *buffers):
    refs = dict(zip(names, buffers), pressure=pressure, residual=residual, coarse=coarse)
    env = KernelEnv(refs)
    cycle(env, [previous[z] for z in range(16)], [divergence[z] for z in range(16)])
    env.finish()


def body(divergence, pressure_prev):
    shapes = scratch()
    block = jax.ShapeDtypeStruct((16, 16, 128), jnp.float32)
    vmem = pl.BlockSpec(memory_space=pltpu.VMEM)
    return pl.pallas_call(
        functools.partial(kernel, tuple(shapes)),
        out_shape=(block, block, jax.ShapeDtypeStruct((4, 4, 32), jnp.float32)),
        in_specs=[vmem, vmem],
        out_specs=(vmem, vmem, vmem),
        scratch_shapes=list(shapes.values()),
        compiler_params=pltpu.CompilerParams(
            collective_id=0, has_side_effects=True, vmem_limit_bytes=48 * 1024 * 1024),
        name="cycle",
    )(divergence, pressure_prev)


def solution(mesh):
    in_specs = (P("gz", "gx", "gy"), P("gz", "gx", "gy"))
    out_specs = (P("gz", "gx", "gy"), P("gz", "gx", "gy"), P())
    return jax.shard_map(body, mesh=mesh, in_specs=in_specs, out_specs=out_specs, check_vma=False)
```

time: 489 us -> 41.4 us (0.08)
  the two profiles are of different devices: /device:TPU:314 before, /device:TPU:1 now
where the time goes in v1:
time: 41.4 us; the launch traced here: 41.2 us
  Pallas kernels  36.9 us (89%)
  local copies, waits for them, and re-layouts  3.71 us (9%)
  between operations  0.65 us (2%)
    pallas_call x1, Pallas kernels, body(): pl.pallas_call(functools.partial(kernel, tuple(shapes)), out_shape=(block...  36.9 us
    unnamed x7, local copies, waits for them, and re-layouts  3.71 us

profile of v1, /device:TPU:1, one launch (start us, length us, event | category | flops | bytes accessed | tf_op | source)
XLA Modules:
  0.0 41.2 jit_solution(17145157335136384425)
XLA Ops:
  0.6 0.0 copy-start
  0.6 0.9 %copy-done = f32[16,16,128]{2,1,0:T(8,128)S(1)} copy-done((f32[16,16,128]{2,1,0:T(8,128)S(1)}, f32[16,16,128]{2,1,0:T(8,128)}, u32[]{:S(2)}) %copy-start) | copy-done | bytes 131096
  1.5 0.0 copy-start.1
  1.5 0.9 %copy-done.1 = f32[16,16,128]{2,1,0:T(8,128)S(1)} copy-done((f32[16,16,128]{2,1,0:T(8,128)S(1)}, f32[16,16,128]{2,1,0:T(8,128)}, u32[]{:S(2)}) %copy-start.1) | copy-done | bytes 131096
  2.4 36.9 %cycle.1 = (f32[16,16,128]{2,1,0:T(8,128)S(1)}, f32[16,16,128]{2,1,0:T(8,128)S(1)}, f32[4,4,32]{2,1,0:T(4,128)S(1)}) custom-call(f32[16,16,128]{2,1,0:T(8,128)S(1)} %copy-done, f32[16,16,128]{2,1,0:T(8,128)S(1)} %copy-done.1), custom_call_target="tpu_custom_call" | custom-call | tf_op jit(solution)/shard_map/cycle/pallas_call | solution.py:566
  39.3 0.7 %copy.8 = f32[16,16,128]{2,1,0:T(8,128)} copy(f32[16,16,128]{2,1,0:T(8,128)S(1)} %get-tuple-element.6) | data formatting | bytes 262144
  40.0 0.7 %copy.9 = f32[16,16,128]{2,1,0:T(8,128)} copy(f32[16,16,128]{2,1,0:T(8,128)S(1)} %get-tuple-element.7) | data formatting | bytes 262144
  40.6 0.6 %copy.10 = f32[4,4,32]{2,1,0:T(4,128)} copy(f32[4,4,32]{2,1,0:T(4,128)S(1)} %get-tuple-element.8) | data formatting | bytes 4096
Async XLA Ops:
  0.6 0.9 %copy-start = (f32[16,16,128]{2,1,0:T(8,128)S(1)}, f32[16,16,128]{2,1,0:T(8,128)}, u32[]{:S(2)}) copy-start(f32[16,16,128]{2,1,0:T(8,128)} %divergence.1) | copy-start | bytes 393220
  1.5 0.9 %copy-start.1 = (f32[16,16,128]{2,1,0:T(8,128)S(1)}, f32[16,16,128]{2,1,0:T(8,128)}, u32[]{:S(2)}) copy-start(f32[16,16,128]{2,1,0:T(8,128)} %previous.1) | copy-start | bytes 393220

commit v2 on v1

--- a/solution.py
+++ b/solution.py
@@ -16,21 +16,25 @@
 OWN = ALPHA - 6.0 * BETA
 
 LANES = 128
+GROUPS2 = ((0, 1, 2), (3, 4), (5, 6, 7))
 RING = 8
 
 SHIFTS = {
-    "x0+": ("gx", 1, 32, 8), "x0-": ("gx", -1, 32, 8),
+    "fx+": ("gx", 1, 1, 16), "fx-": ("gx", -1, 1, 16),
+    "fz+": ("gz", 1, 1, 16), "fz-": ("gz", -1, 1, 16),
+    "fy+": ("gy", 1, 1, 16), "fy-": ("gy", -1, 1, 16),
+    "x0+": ("gx", 1, 8, 8), "x0-": ("gx", -1, 8, 8),
     "x1+": ("gx", 1, 12, 8), "x1-": ("gx", -1, 12, 8),
-    "x2+1": ("gx", 1, 8, 8), "x2-1": ("gx", -1, 8, 8),
-    "x2+2": ("gx", 2, 8, 8), "x2-2": ("gx", -2, 8, 8),
-    "z0+": ("gz", 1, 9, 32), "z0-": ("gz", -1, 9, 32),
+    "x2+1": ("gx", 1, 3, 8), "x2-1": ("gx", -1, 3, 8),
+    "x2+2": ("gx", 2, 3, 8), "x2-2": ("gx", -2, 3, 8),
+    "z0+": ("gz", 1, 4, 24), "z0-": ("gz", -1, 4, 24),
     "z1+": ("gz", 1, 7, 24), "z1-": ("gz", -1, 7, 24),
-    "z2+1": ("gz", 1, 7, 16), "z2-1": ("gz", -1, 7, 16),
-    "z2+2": ("gz", 2, 3, 16), "z2-2": ("gz", -2, 3, 16),
-    "y0+": ("gy", 1, 4, 32), "y0-": ("gy", -1, 4, 32),
+    "z2+1": ("gz", 1, 3, 16), "z2-1": ("gz", -1, 3, 16),
+    "z2+2": ("gz", 2, 1, 16), "z2-2": ("gz", -2, 1, 16),
+    "y0+": ("gy", 1, 1, 24), "y0-": ("gy", -1, 1, 24),
     "y1+": ("gy", 1, 2, 24), "y1-": ("gy", -1, 2, 24),
     "y2+": ("gy", 1, 1, 16), "y2-": ("gy", -1, 1, 16),
-    "y3+": ("gy", 1, 4, 16), "y3-": ("gy", -1, 4, 16),
+    "y3+": ("gy", 1, 1, 16), "y3-": ("gy", -1, 1, 16),
 }
 GATHERS = {"gx3": ("gx", 8), "gz3": ("gz", 16), "gy4": ("gy", 8)}
 
@@ -146,24 +150,23 @@
             return mask(z) * out
         return Field(lo, hi, make)
 
-    def slots(self, rows, start):
-        lane = (iota((rows, LANES), 1) - start) % LANES
-        return number(lane < 8)
-
-    def pack(self, planes, start):
-        rows = planes[0].shape[0]
+    def slots(self, rows, start, width):
+        lane = (iota((rows, LANES), 1) - start) & (LANES - 1)
+        return number(lane < width)
+
+    def pack(self, planes, start, width=8):
+        rows, per = planes[0].shape[0], LANES // width
         tiles = []
-        for g in range(0, len(planes), 16):
-            tile = None
-            for w, plane in enumerate(planes[g:g + 16]):
-                part = self.slots(rows, 8 * w) * self.roll(plane, 8 * w - start, 1)
-                tile = part if tile is None else tile + part
-            tiles.append(tile)
+        for g in range(0, len(planes), per):
+            tiles.append(total([
+                self.slots(rows, width * w, width) * self.roll(plane, width * w - start, 1)
+                for w, plane in enumerate(planes[g:g + per])
+            ]))
         return tiles
 
-    def unpack(self, tiles, count, start):
-        keep = self.slots(tiles[0].shape[0], start)
-        return [keep * self.roll(tiles[i // 16], start - 8 * (i % 16), 1) for i in range(count)]
+    def unpack(self, tiles, count, start, width=8):
+        keep, per = self.slots(tiles[0].shape[0], start, width), LANES // width
+        return [keep * self.roll(tiles[i // per], start - width * (i % per), 1) for i in range(count)]
 
 
 def cycle(env, x_own, b_own):
@@ -205,12 +208,44 @@
 
     env.ready()
     env.gather_send("gx3", b3c)
+    env.shift_send("fx+", [env.row(x_own, 15)])
+    env.shift_send("fx-", [env.row(x_own, 0)])
+    env.shift_send("fz+", [x_own[15]])
+    env.shift_send("fz-", [x_own[0]])
+    lane16 = iota((16, LANES), 1)
+    env.shift_send("fy+", m.pack(x_own, 127, 1))
+    env.shift_send("fy-", m.pack(x_own, 0, 1))
+    packed2 = [total([m.roll(b2c[i], 40 * w + 2, 1) for w, i in enumerate(g)]) for g in GROUPS2]
     for d in (1, -1, 2, -2):
-        env.shift_send("x2%+d" % d, b2c)
+        env.shift_send("x2%+d" % d, packed2)
     env.shift_send("x1+", [m.take_rows(b1c(z), 7, 8) for z in range(-2, 10)])
     env.shift_send("x1-", [m.take_rows(b1c(z), 2, 8) for z in range(-2, 10)])
-    env.shift_send("x0+", [v[8:] for v in x_own] + [v[8:] for v in b_own])
-    env.shift_send("x0-", [v[:8] for v in x_own] + [v[:8] for v in b_own])
+
+    row_a, lane_a = iota((16, LANES), 0), iota((16, LANES), 1)
+    inside = lambda at: (number(at > 0), number(at < RING - 1))
+    (z_lo, z_hi), (x_lo, x_hi), (y_lo, y_hi) = inside(iz), inside(ix), inside(iy)
+    row_first, row_last = x_lo * number(row_a == 0), x_hi * number(row_a == 15)
+    row_later, row_sooner = number(row_a > 0), number(row_a < 15)
+    y_first, y_last = y_lo * number(lane_a == 0), y_hi * number(lane_a == 127)
+    y_later, y_sooner = number(lane_a > 0), number(lane_a < 127)
+    fx_lo, fx_hi = env.shift_recv("fx+")[0], env.shift_recv("fx-")[0]
+    fz_lo, fz_hi = z_lo * env.shift_recv("fz+")[0], z_hi * env.shift_recv("fz-")[0]
+    fy_lo, fy_hi = env.shift_recv("fy+")[0], env.shift_recv("fy-")[0]
+    r_own = []
+    for z in range(16):
+        v = x_own[z]
+        near = (x_own[z - 1] if z else fz_lo) + (x_own[z + 1] if z < 15 else fz_hi)
+        near = near + row_later * m.roll(v, 1, 0) + row_first * fx_lo[z:z + 1]
+        near = near + row_sooner * m.roll(v, -1, 0) + row_last * fx_hi[z:z + 1]
+        near = near + y_later * m.roll(v, 1, 1) + y_first * m.roll(fy_lo, -z, 1)
+        near = near + y_sooner * m.roll(v, -1, 1) + y_last * m.roll(fy_hi, 127 - z, 1)
+        r_own.append(b_own[z] - 6.0 * v + near)
+    row8 = iota((8, LANES), 0)
+    is_low = row8 < 4
+    two = lambda a, b: jnp.where(is_low, a, b)
+    half = lambda v: m.roll(v, 4, 0)
+    env.shift_send("x0+", [two(half(r_own[2 * i][8:]), r_own[2 * i + 1][8:]) for i in range(8)])
+    env.shift_send("x0-", [two(r_own[2 * i][:8], half(r_own[2 * i + 1][:8])) for i in range(8)])
 
     parts = env.gather_recv("gx3")
     wide = total([m.place_rows(v, 2 * k, 24) for k, v in enumerate(parts)])
@@ -218,18 +253,30 @@
 
     env.gather_send("gz3", b3x)
 
+    before, after = env.shift_recv("x0+"), env.shift_recv("x0-")
+    r0x = []
+    for z in range(16):
+        low, high = half(r_own[z][:8]), half(r_own[z][8:])
+        lo, hi = before[z // 2], after[z // 2]
+        if z % 2:
+            lo = half(lo)
+        else:
+            hi = half(hi)
+        r0x.append(jnp.concatenate([two(lo, low), two(low, high), two(high, hi)], axis=0))
+    env.shift_send("z0+", r0x[12:])
+    env.shift_send("z0-", r0x[:4])
+
     got = {d: env.shift_recv("x2%+d" % d) for d in (1, -1, 2, -2)}
-    row8 = iota((8, LANES), 0)
     low, high = number(row8 < 4), number(row8 >= 4)
     b2x = []
-    for i in range(8):
-        lo = got[1][i] + low * m.roll(got[2][i], 4, 0)
-        hi = got[-1][i] + high * m.roll(got[-2][i], 4, 0)
-        b2x.append(jnp.concatenate([lo, hi], axis=0) + m.place_rows(b2c[i], 4, 16))
-    env.shift_send("z2+1", b2x[1:])
-    env.shift_send("z2-1", b2x[:7])
-    env.shift_send("z2+2", b2x[5:])
-    env.shift_send("z2-2", b2x[:3])
+    for i in range(3):
+        lo = got[1][i] + low * half(got[2][i])
+        hi = got[-1][i] + high * half(got[-2][i])
+        b2x.append(jnp.concatenate([lo, hi], axis=0) + m.place_rows(packed2[i], 4, 16))
+    env.shift_send("z2+1", b2x)
+    env.shift_send("z2-1", b2x)
+    env.shift_send("z2+2", b2x[2:])
+    env.shift_send("z2-2", b2x[:1])
 
     before, after = env.shift_recv("x1+"), env.shift_recv("x1-")
     b1x = [
@@ -239,12 +286,9 @@
     env.shift_send("z1+", b1x[5:])
     env.shift_send("z1-", b1x[:7])
 
-    before, after = env.shift_recv("x0+"), env.shift_recv("x0-")
-    own = x_own + b_own
-    joined = [jnp.concatenate([before[i], own[i], after[i]], axis=0) for i in range(32)]
-    x0x, b0x = joined[:16], joined[16:]
-    env.shift_send("z0+", x0x[11:] + b0x[12:])
-    env.shift_send("z0-", x0x[:5] + b0x[:4])
+    r0w = env.shift_recv("z0+") + r0x + env.shift_recv("z0-")
+    env.shift_send("y0+", m.pack(r0w, 124, 4))
+    env.shift_send("y0-", m.pack(r0w, 0, 4))
 
     parts = env.gather_recv("gz3")
     lane = iota((16, LANES), 1)
@@ -283,24 +327,34 @@
     b4c = dot(halve_rows, dot(p3, gather_lanes))
 
     env.gather_send("gy4", b4c)
-    env.shift_send("y3+", lanes_of(b3s))
-    env.shift_send("y3-", lanes_of(b3s))
+    octet = (lane >> 3) & 3
+    squeeze = lambda at: total([
+        number(octet == q) * m.roll(v, 8 * q - at, 1) for q, v in enumerate(lanes_of(b3s))
+    ])
+    env.shift_send("y3+", [squeeze(19)])
+    env.shift_send("y3-", [squeeze(6)])
 
     got = {d: env.shift_recv("z2%+d" % d) for d in (1, -1, 2, -2)}
+    keep = m.slots(16, 126, 40)
+
+    def plane2(groups, i):
+        g = [i in group for group in GROUPS2].index(True)
+        return m.roll(groups[g], -(40 * GROUPS2[g].index(i) + 2), 1)
+
     b2w = []
     for z in range(-5, 9):
         here = []
         if -2 <= z <= 5:
-            here.append(b2x[z + 2])
+            here.append(plane2(b2x, z + 2))
         if z <= 1:
-            here.append(got[1][z + 5])
+            here.append(plane2(got[1], z + 6))
         if z >= 2:
-            here.append(got[-1][z - 2])
+            here.append(plane2(got[-1], z - 2))
         if z <= -3:
-            here.append(got[2][z + 5])
+            here.append(plane2([None, None] + got[2], z + 10))
         if z >= 6:
-            here.append(got[-2][z - 6])
-        b2w.append(total(here))
+            here.append(plane2(got[-2], z - 6))
+        b2w.append(keep * total(here))
     env.shift_send("y2+", m.pack(b2w, 27))
     env.shift_send("y2-", m.pack(b2w, 126))
 
@@ -318,11 +372,23 @@
     env.shift_send("y1+", m.pack(b1w, 59))
     env.shift_send("y1-", m.pack(b1w, 126))
 
-    before, after = env.shift_recv("z0+"), env.shift_recv("z0-")
-    x0w = before[:5] + x0x + after[:5]
-    b0w = before[5:] + b0x + after[5:]
-    env.shift_send("y0+", m.pack(x0w, 120) + m.pack(b0w, 120))
-    env.shift_send("y0-", m.pack(x0w, 0) + m.pack(b0w, 0))
+    before, after = env.shift_recv("y3+")[0], env.shift_recv("y3-")[0]
+    slot16 = lane16 & 31
+    low_slot, high_slot = number((slot16 >= 3) & (slot16 < 11)), number((slot16 >= 22) & (slot16 < 30))
+    b3w = mask3 * (b3s + jnp.concatenate([
+        low_slot * m.roll(before, 3 - 8 * q, 1) + high_slot * m.roll(after, 22 - 8 * q, 1) for q in range(4)
+    ], axis=1))
+    u3 = correction3(b3w)
+    p3 = minus_op3(b3w, u3)
+
+    mask0 = m.mask(0, 24, 4, 256, 128)
+    low = m.unpack(env.shift_recv("y0+"), 24, 124, 4)
+    high = m.unpack(env.shift_recv("y0-"), 24, 0, 4)
+    r0 = field_of(-4, [
+        mask0(i - 4) * jnp.concatenate([v, low[i] + high[i]], axis=1) for i, v in enumerate(r0w)
+    ])
+    u0 = m.correction(r0, mask0, -3, 18)
+    p0 = m.minus_op(r0, u0, mask0, -2, 17)
 
     parts = env.gather_recv("gy4")
     row, lane = iota((8, LANES), 0), iota((8, LANES), 1)
@@ -381,12 +447,6 @@
     planes = right(e4, own_y)
     wide = jnp.concatenate([planes[2 * k] + m.roll(planes[2 * k + 1], 64, 1) for k in range(4)], axis=1)
     c3 = mask3 * dot(select_matrix((16, 8), lambda a, c: (a >> 1) == c), wide)
-    before = jnp.concatenate(env.shift_recv("y3+"), axis=1)
-    after = jnp.concatenate(env.shift_recv("y3-"), axis=1)
-    b3w = b3s + number((slot >= 3) & (slot < 10)) * m.roll(before, -16, 1)
-    b3w = mask3 * (b3w + number((slot >= 22) & (slot < 29)) * m.roll(after, 16, 1))
-    u3 = correction3(b3w)
-    p3 = minus_op3(b3w, u3)
     e3 = u3 + c3 + correction3(minus_op3(p3, c3))
 
     spread = select_matrix((16, 16), lambda a, c: 2 * ix + ((a - 6) >> 1) == c)
@@ -423,30 +483,15 @@
     v1 = m.correction(m.minus_op(p1, c1, mask1, -3, 10), mask1, -2, 9)
     e1 = [u1(z) + mask1(z) * c1(z) + v1(z) for z in range(-2, 10)]
 
-    coarse = left(select_matrix((32, 24), lambda a, c: (a >> 1) + 4 == c), e1)
+    coarse = left(select_matrix((24, 24), lambda a, c: ((a - 4) >> 1) + 8 == c), e1)
     coarse = right(coarse, select_matrix((128, 256), lambda a, c: a == (c >> 1)))
     c0 = field_of(-4, [coarse[(z >> 1) + 2] for z in range(-4, 20)])
-    mask0 = m.mask(0, 32, 8, 256, 128)
-    before, after = env.shift_recv("y0+"), env.shift_recv("y0-")
-
-    def window0(planes, lo, some):
-        low = m.unpack(before[some], len(planes), 120)
-        high = m.unpack(after[some], len(planes), 0)
-        return field_of(lo, [
-            mask0(lo + i) * jnp.concatenate([v, low[i] + high[i]], axis=1) for i, v in enumerate(planes)
-        ])
-
-    x0 = window0(x0w, -5, slice(0, 2))
-    b0 = window0(b0w, -4, slice(2, 4))
-    r0 = m.minus_op(b0, x0, mask0, -4, 19)
-    u0 = m.correction(r0, mask0, -3, 18)
-    p0 = m.minus_op(r0, u0, mask0, -2, 17)
     q0 = m.minus_op(p0, c0, mask0, -2, 17)
     v0 = m.correction(q0, mask0, -1, 16)
     left_over = m.minus_op(q0, v0, mask0, 0, 15)
-    inner = lambda v: v[8:24, :LANES]
+    inner = lambda v: m.take_rows(v[:, :LANES], 4, 16)
     for z in range(16):
-        env.fine_out(z, x_own[z] + inner(u0(z)) + inner(c0(z)) + inner(v0(z)), inner(left_over(z)))
+        env.fine_out(z, x_own[z] + inner(u0(z) + c0(z) + v0(z)), inner(left_over(z)))
 
 
 class KernelEnv:
@@ -467,6 +512,9 @@
     def roll(self, v, shift, axis):
         return pltpu.roll(v, shift, axis)
 
+    def row(self, planes, x):
+        return self.refs["previous"][pl.ds(x, 16, stride=16), :]
+
     def ready(self):
         pl.semaphore_wait(self.barrier, 3 * (RING - 1))
 
@@ -501,7 +549,7 @@
         me = self.at[axis]
         buf, src, sems = self.refs["in" + name], self.refs["out" + name], self.refs["gather_sems"]
         src[...] = v
-        for d in (1, 7, 2, 6, 3, 5, 4):
+        for d in (4, 3, 5, 2, 6, 1, 7):
             copy = self.copy(src, buf.at[me], sems.at[0, i, d], sems.at[1, i, me], axis, d)
             copy.start()
             self.started.append(copy)
@@ -546,6 +594,9 @@
     for name, (_, rows) in GATHERS.items():
         shapes["out" + name] = pltpu.VMEM((rows, LANES), jnp.float32)
         shapes["in" + name] = pltpu.VMEM((RING, rows, LANES), jnp.float32)
+    shapes["previous"] = pltpu.VMEM((256, LANES), jnp.float32)
+    shapes["divergence"] = pltpu.VMEM((256, LANES), jnp.float32)
+    shapes["load_sems"] = pltpu.SemaphoreType.DMA((2,))
     shapes["planes3"] = pltpu.VMEM((20, 16, LANES), jnp.float32)
     shapes["shift_sems"] = pltpu.SemaphoreType.DMA((2, len(SHIFTS)))
     shapes["gather_sems"] = pltpu.SemaphoreType.DMA((2, len(GATHERS), RING))
@@ -554,25 +605,53 @@
 
 def kernel(names, divergence, previous, pressure, residual, coarse, *buffers):
     refs = dict(zip(names, buffers), pressure=pressure, residual=residual, coarse=coarse)
+    loads = [
+        pltpu.make_async_copy(previous, refs["previous"], refs["load_sems"].at[0]),
+        pltpu.make_async_copy(divergence, refs["divergence"], refs["load_sems"].at[1]),
+    ]
+    for load in loads:
+        load.start()
     env = KernelEnv(refs)
-    cycle(env, [previous[z] for z in range(16)], [divergence[z] for z in range(16)])
+    for load in loads:
+        load.wait()
+    planes = lambda name: [refs[name][16 * z:16 * z + 16] for z in range(16)]
+    cycle(env, planes("previous"), planes("divergence"))
     env.finish()
+
+
+def store_kernel(*refs):
+    values, outs, sems = refs[:3], refs[3:6], refs[6]
+    copies = [pltpu.make_async_copy(v, o, sems.at[i]) for i, (v, o) in enumerate(zip(values, outs))]
+    for copy in copies:
+        copy.start()
+    for copy in copies:
+        copy.wait()
 
 
 def body(divergence, pressure_prev):
     shapes = scratch()
     block = jax.ShapeDtypeStruct((16, 16, 128), jnp.float32)
-    vmem = pl.BlockSpec(memory_space=pltpu.VMEM)
-    return pl.pallas_call(
+    outs = (block, block, jax.ShapeDtypeStruct((4, 4, 32), jnp.float32))
+    vmem, hbm = pl.BlockSpec(memory_space=pltpu.VMEM), pl.BlockSpec(memory_space=pltpu.HBM)
+    results = pl.pallas_call(
         functools.partial(kernel, tuple(shapes)),
-        out_shape=(block, block, jax.ShapeDtypeStruct((4, 4, 32), jnp.float32)),
-        in_specs=[vmem, vmem],
+        out_shape=outs,
+        in_specs=[hbm, hbm],
         out_specs=(vmem, vmem, vmem),
         scratch_shapes=list(shapes.values()),
         compiler_params=pltpu.CompilerParams(
             collective_id=0, has_side_effects=True, vmem_limit_bytes=48 * 1024 * 1024),
         name="cycle",
-    )(divergence, pressure_prev)
+    )(*(pltpu.with_memory_space_constraint(v.reshape(256, 128), pltpu.HBM) for v in (divergence, pressure_prev)))
+    return pl.pallas_call(
+        store_kernel,
+        out_shape=outs,
+        in_specs=[vmem, vmem, vmem],
+        out_specs=(hbm, hbm, hbm),
+        scratch_shapes=[pltpu.SemaphoreType.DMA((3,))],
+        compiler_params=pltpu.CompilerParams(vmem_limit_bytes=1024 * 1024),
+        name="store",
+    )(*results)
 
 
 def solution(mesh):

time: 41.4 us -> 38.8 us (0.937)
  local copies, waits for them, and re-layouts: 3.71 us -> 0 us
  Pallas kernels: 36.9 us -> 38 us
    unnamed x7 -> x0, local copies, waits for them, and re-layouts: 3.71 us -> none
    pallas_call x1 -> x2, Pallas kernels: 36.9 us -> 38 us  [the longest x1 37.3 us: body(): pl.pallas_call(functools.partial(kernel, tuple(shapes)), out_shape=outs,...]
where the time goes in v2:
time: 38.8 us; the launch traced here: 38.6 us
  Pallas kernels  38 us (98%)
  between operations  0.64 us (2%)
    pallas_call x1, Pallas kernels, body(): pl.pallas_call(functools.partial(kernel, tuple(shapes)), out_shape=outs,...  37.3 us

profile of v2, /device:TPU:1, one launch (start us, length us, event | category | flops | bytes accessed | tf_op | source)
XLA Modules:
  0.0 38.6 jit_solution(7300780928975967527)
XLA Ops:
  0.6 37.3 %cycle.1 = (f32[16,16,128]{2,1,0:T(8,128)S(1)}, f32[16,16,128]{2,1,0:T(8,128)S(1)}, f32[4,4,32]{2,1,0:T(4,128)S(1)}) custom-call(f32[256,128]{1,0:T(8,128)} %bitcast.2, f32[256,128]{1,0:T(8,128)} %bitcast.3), custom_call_target="tpu_custom_call" | custom-call | tf_op jit(solution)/shard_map/cycle/pallas_call | solution.py:636
  37.9 0.7 %store.1 = (f32[16,16,128]{2,1,0:T(8,128)}, f32[16,16,128]{2,1,0:T(8,128)}, f32[4,4,32]{2,1,0:T(4,128)}) custom-call(f32[16,16,128]{2,1,0:T(8,128)S(1)} %get-tuple-element.6.refs_0_, f32[16,16,128]{2,1,0:T(8,128)S(1)} %get-tuple-element.7.refs_1_, f32[4,4,32]{2,1,0:T(4,128)S(1)} %get-tuple-element.8.refs_2_), custom_call_target="tpu_custom_call" | custom-call | tf_op jit(solution)/shard_map/store/pallas_call | solution.py:646

commit v3 on v2

--- a/solution.py
+++ b/solution.py
@@ -39,6 +39,16 @@
 GATHERS = {"gx3": ("gx", 8), "gz3": ("gz", 16), "gy4": ("gy", 8)}
 
 
+KEPT = {
+    "s0": (16, 16, 128), "p0": (20, 24, 256), "u1": (12, 24, 128), "p1": (14, 24, 128),
+    "u2": (8, 16, 128), "p2": (10, 16, 128), "u3": (1, 16, 512), "p3": (1, 16, 512),
+}
+MATRICES = {
+    "lanes3": (512, 128), "lanes4": (128, 128), "up5": (128, 128), "up4": (128, 128), "up3": (128, 128),
+    "up2": (128, 128), "up1": (128, 256), "next3": (128, 128), "next2": (128, 128), "next1": (128, 256),
+}
+
+
 def iota(shape, dim):
     return lax.broadcasted_iota(jnp.int32, shape, dim)
 
@@ -47,12 +57,29 @@
     return jnp.where(cond, 1.0, 0.0).astype(jnp.float32)
 
 
-def dot(a, b):
-    return jnp.dot(a, b, precision=lax.Precision.HIGHEST, preferred_element_type=jnp.float32)
+def parts_of(v):
+    high = v.astype(jnp.bfloat16)
+    return high, (v - high.astype(jnp.float32)).astype(jnp.bfloat16)
+
+
+def product(a, b):
+    return jnp.dot(a, b, preferred_element_type=jnp.float32)
+
+
+def times(v, matrix):
+    high, low = parts_of(v)
+    if v.shape[1] == LANES:
+        return product(jnp.concatenate([high, low], axis=1), jnp.concatenate([matrix, matrix], axis=0))
+    return product(high, matrix) + product(low, matrix)
+
+
+def onto(matrix, v):
+    high, low = parts_of(v)
+    return product(matrix, high) + product(matrix, low)
 
 
 def select_matrix(shape, hit, value=1.0):
-    return number(hit(iota(shape, 0), iota(shape, 1))) * value
+    return jnp.where(hit(iota(shape, 0), iota(shape, 1)), value, 0.0).astype(jnp.bfloat16)
 
 
 def rows_of(stacked, rows):
@@ -64,11 +91,25 @@
 
 
 def right(planes, matrix):
-    return rows_of(dot(jnp.concatenate(planes, axis=0), matrix), planes[0].shape[0])
+    return rows_of(times(jnp.concatenate(planes, axis=0), matrix), planes[0].shape[0])
 
 
 def left(matrix, planes):
-    return lanes_of(dot(matrix, jnp.concatenate(planes, axis=1)))
+    return lanes_of(onto(matrix, jnp.concatenate(planes, axis=1)))
+
+
+def widen(own, beside, rows, up, following):
+    (own_high, own_low), (beside_high, beside_low) = parts_of(own), parts_of(beside)
+    join = lambda a, b: jnp.concatenate([a, b], axis=1)
+    inner = product(join(own_high, own_low), jnp.concatenate([up, up], axis=0))
+    both = jnp.concatenate([up, following], axis=0)
+    outer = product(join(beside_high, own_high), both) + product(join(beside_low, own_low), both)
+    return rows_of(inner, rows), rows_of(outer, rows)
+
+
+def halves(planes):
+    rows = planes[0].shape[0] // 2
+    return jnp.concatenate([v[:rows] for v in planes], axis=0), jnp.concatenate([v[rows:] for v in planes], axis=0), rows
 
 
 def total(terms):
@@ -147,7 +188,13 @@
                 out = out - 6.0 * x(z)
             if b(z) is not None:
                 out = out + b(z)
-            return mask(z) * out
+            return out if mask is None else mask(z) * out
+        return Field(lo, hi, make)
+
+    def minus_op_of_coarse(self, b, inner, outer, lo_coarse, mask, lo, hi):
+        def make(z):
+            at = (z >> 1) - lo_coarse
+            return mask(z) * (b(z) + outer[at] + inner[at + 2 * (z & 1) - 1] - 3.0 * inner[at])
         return Field(lo, hi, make)
 
     def slots(self, rows, start, width):
@@ -169,9 +216,59 @@
         return [keep * self.roll(tiles[i // per], start - width * (i % per), 1) for i in range(count)]
 
 
-def cycle(env, x_own, b_own):
+class Selections:
+    def __init__(self, ix, iy):
+        self.lanes0 = select_matrix((256, 128), lambda a, c: (a >> 1) == c, 0.5)
+        self.rows0 = select_matrix((16, 24), lambda a, c: (c >> 1) + 2 == a)
+        self.lanes1 = select_matrix((128, 128), lambda a, c: (a >> 1) + jnp.where(a >= 96, 64, 0) == c, 0.5)
+        self.halve_rows = select_matrix((8, 16), lambda a, c: (c >> 1) == a)
+        self.lanes2 = select_matrix((128, 128), lambda a, c: (jnp.where(a < 80, a, a - 128) >> 1) + 2 == c, 0.5)
+        self.ix, self.iy = ix, iy
+
+    def rest(self, env):
+        ix, iy = self.ix, self.iy
+        y_of = lambda c: jnp.where(c < 80, c, c - 128)
+        y_fine = lambda c: jnp.where(c < 96, c, c - 128)
+        side = lambda c: 2 * (c & 1) - 1
+
+        def up_rows(rows, depth, coarse):
+            fine = lambda a: jnp.where(a >= rows, a - rows, a)
+            return select_matrix((2 * rows, depth), lambda a, c: (
+                coarse(fine(a)) + jnp.where(a >= rows, side(fine(a)), 0) == c))
+
+        hits = {
+            "lanes3": lambda a, c: 16 * (a >> 6) + ((a & 31) >> 1) == c,
+            "lanes4": lambda a, c: ((a >> 1) == c) & (a < 64),
+            "up5": lambda a, c: (a == (c >> 1)) & (c < 64),
+            "up4": lambda a, c: (a == 8 * iy + (((c & 31) - 8) >> 1)) & (c < 64),
+            "up3": lambda a, c: (a - 8 == (y_of(c) >> 1)) & (a < 32) & (y_of(c) < 36) & (y_of(c) >= -4),
+            "up2": lambda a, c: y_of(a) == (y_fine(c) >> 1),
+            "up1": lambda a, c: a == (c >> 1),
+            "next3": lambda a, c: (
+                (a - 8 == (y_of(c) >> 1) + side(c)) & (a < 32) & (y_of(c) < 36) & (y_of(c) >= -4)),
+            "next2": lambda a, c: y_of(a) == (y_fine(c) >> 1) + side(c),
+            "next1": lambda a, c: a == (((c >> 1) + side(c)) & 127),
+        }
+        for name, hit in hits.items():
+            value = 0.5 if name.startswith("lanes") else 1.0
+            env.keep_matrix(name, select_matrix(MATRICES[name], hit, value))
+        self.env = env
+        self.rows4 = select_matrix((16, 32), lambda a, c: (c >> 3) * 4 + ((c & 7) >> 1) == a)
+        self.up_rows5 = select_matrix((32, 16), lambda a, c: (a >> 3) * 4 + ((a & 7) >> 1) == c)
+        self.up_rows4 = select_matrix((16, 8), lambda a, c: (a >> 1) == c)
+        self.up_rows3 = up_rows(16, 16, lambda a: 2 * ix + ((a - 6) >> 1))
+        self.up_rows2 = up_rows(24, 16, lambda a: (a >> 1) + 2)
+        self.up_rows1 = up_rows(24, 24, lambda a: ((a - 4) >> 1) + 8)
+
+    def kept(self, name):
+        return self.env.matrix(name)
+
+
+def cycle(env):
     m = Math(env)
     iz, ix, iy = env.position
+    pick = Selections(ix, iy)
+    x_own, b_own = env.load()
     zeros = lambda *s: jnp.zeros(s, jnp.float32)
 
     mask0 = m.mask(0, 24, 4, 256, 128)
@@ -180,30 +277,26 @@
     bc = Field(0, 15, lambda z: put0(b_own[z]))
     r0 = m.minus_op(bc, xc, mask0, -1, 16)
     u0 = m.correction(r0, mask0, -2, 17)
-    p0 = m.minus_op(r0, u0, mask0, -3, 18)
+    p0 = m.minus_op(r0, u0, None, -3, 18)
     coarse = [total([p0(2 * z), p0(2 * z + 1)]) for z in range(-2, 10)]
-    coarse = right(coarse, select_matrix((256, 128), lambda a, c: (a >> 1) == c, 0.5))
-    coarse = left(select_matrix((16, 24), lambda a, c: (c >> 1) + 2 == a), coarse)
+    coarse = right(coarse, pick.lanes0)
+    coarse = left(pick.rows0, coarse)
     mask1c = m.mask(1, 16, 4, 128, 64)
     b1c = field_of(-2, [mask1c(z) * v for z, v in zip(range(-2, 10), coarse)])
 
     u1 = m.correction(b1c, mask1c, -3, 10)
-    p1 = m.minus_op(b1c, u1, mask1c, -4, 11)
+    p1 = m.minus_op(b1c, u1, None, -4, 11)
     coarse = [total([p1(2 * z), p1(2 * z + 1)]) for z in range(-2, 6)]
-    half = select_matrix((128, 128), lambda a, c: (a >> 1) + jnp.where(a >= 96, 64, 0) == c, 0.5)
-    coarse = right(coarse, half)
-    halve_rows = select_matrix((8, 16), lambda a, c: (c >> 1) == a)
-    coarse = left(halve_rows, coarse)
+    coarse = left(pick.halve_rows, right(coarse, pick.lanes1))
     mask2e = m.mask(2, 8, 2, 128, 32)
     b2c = [mask2e(z) * v for z, v in zip(range(-2, 6), coarse)]
 
     mask2c = m.mask(2, 16, 4, 128, 32)
     b2p = field_of(-2, [m.place_rows(v, 2, 16) for v in b2c])
     u2 = m.correction(b2p, mask2c, -3, 6)
-    p2 = m.minus_op(b2p, u2, mask2c, -4, 7)
+    p2 = m.minus_op(b2p, u2, None, -4, 7)
     coarse = [total([p2(2 * z), p2(2 * z + 1)]) for z in range(-2, 4)]
-    half = select_matrix((128, 128), lambda a, c: (jnp.where(a < 80, a, a - 128) >> 1) + 2 == c, 0.5)
-    coarse = left(halve_rows, right(coarse, half))
+    coarse = left(pick.halve_rows, right(coarse, pick.lanes2))
     b3c = total([m.roll(v, 20 * s, 1) for s, v in enumerate(coarse)])
 
     env.ready()
@@ -247,6 +340,8 @@
     env.shift_send("x0+", [two(half(r_own[2 * i][8:]), r_own[2 * i + 1][8:]) for i in range(8)])
     env.shift_send("x0-", [two(r_own[2 * i][:8], half(r_own[2 * i + 1][:8])) for i in range(8)])
 
+    pick.rest(env)
+
     parts = env.gather_recv("gx3")
     wide = total([m.place_rows(v, 2 * k, 24) for k, v in enumerate(parts)])
     b3x = m.take_rows(wide, 2, 16)
@@ -323,8 +418,7 @@
 
     b3s = mask3 * jnp.concatenate(tiles, axis=1)
     p3 = minus_op3(b3s, correction3(b3s))
-    gather_lanes = select_matrix((512, 128), lambda a, c: 16 * (a >> 6) + ((a & 31) >> 1) == c, 0.5)
-    b4c = dot(halve_rows, dot(p3, gather_lanes))
+    b4c = onto(pick.halve_rows, times(p3, pick.kept("lanes3")))
 
     env.gather_send("gy4", b4c)
     octet = (lane >> 3) & 3
@@ -372,6 +466,18 @@
     env.shift_send("y1+", m.pack(b1w, 59))
     env.shift_send("y1-", m.pack(b1w, 126))
 
+    mask0 = m.mask(0, 24, 4, 256, 128)
+    low = m.unpack(env.shift_recv("y0+"), 24, 124, 4)
+    high = m.unpack(env.shift_recv("y0-"), 24, 0, 4)
+    r0 = field_of(-4, [
+        mask0(i - 4) * jnp.concatenate([v, low[i] + high[i]], axis=1) for i, v in enumerate(r0w)
+    ])
+    u0 = m.correction(r0, mask0, -3, 18)
+    p0 = m.minus_op(r0, u0, None, -2, 17)
+    p0 = Field(-2, 17, env.keep("p0", -2, p0))
+    near_x = Field(0, 15, lambda z: x_own[z] + m.take_rows(u0(z)[:, :LANES], 4, 16))
+    s0 = env.keep("s0", 0, near_x)
+
     before, after = env.shift_recv("y3+")[0], env.shift_recv("y3-")[0]
     slot16 = lane16 & 31
     low_slot, high_slot = number((slot16 >= 3) & (slot16 < 11)), number((slot16 >= 22) & (slot16 < 30))
@@ -380,15 +486,28 @@
     ], axis=1))
     u3 = correction3(b3w)
     p3 = minus_op3(b3w, u3)
-
-    mask0 = m.mask(0, 24, 4, 256, 128)
-    low = m.unpack(env.shift_recv("y0+"), 24, 124, 4)
-    high = m.unpack(env.shift_recv("y0-"), 24, 0, 4)
-    r0 = field_of(-4, [
-        mask0(i - 4) * jnp.concatenate([v, low[i] + high[i]], axis=1) for i, v in enumerate(r0w)
-    ])
-    u0 = m.correction(r0, mask0, -3, 18)
-    p0 = m.minus_op(r0, u0, mask0, -2, 17)
+    early_u3, early_p3 = u3, p3
+    u3, p3 = env.keep("u3", 0, lambda z: early_u3), env.keep("p3", 0, lambda z: early_p3)
+
+    def window(level, planes, tag, rows, row_off, lo, own_y, at_low, at_high):
+        mask = m.mask(level, rows, row_off, LANES, own_y)
+        before = m.unpack(env.shift_recv(tag + "+"), len(planes), at_low)
+        after = m.unpack(env.shift_recv(tag + "-"), len(planes), at_high)
+        return mask, field_of(lo, [
+            mask(lo + i) * (v + before[i] + after[i]) for i, v in enumerate(planes)
+        ])
+
+    mask2, b2 = window(2, b2w, "y2", 16, 6, -5, 32, 123, 30)
+    u2 = m.correction(b2, mask2, -4, 7)
+    p2 = m.minus_op(b2, u2, None, -3, 6)
+    p2 = Field(-3, 6, env.keep("p2", -3, p2))
+    u2 = env.keep("u2", -2, u2)
+    mask1, b1 = window(1, b1w, "y1", 24, 8, -5, 64, 123, 62)
+    u1 = m.correction(b1, mask1, -4, 11)
+    p1 = m.minus_op(b1, u1, None, -3, 10)
+    p1 = Field(-3, 10, env.keep("p1", -3, p1))
+    u1 = env.keep("u1", -2, u1)
+    env.flush()
 
     parts = env.gather_recv("gy4")
     row, lane = iota((8, LANES), 0), iota((8, LANES), 1)
@@ -416,9 +535,8 @@
 
     u4 = correction4(b4)
     p4 = minus_op4(b4, u4)
-    half = select_matrix((128, 128), lambda a, c: ((a >> 1) == c) & (a < 64), 0.5)
     coarse = jnp.concatenate([p4(2 * z) + p4(2 * z + 1) for z in range(4)], axis=0)
-    b5 = dot(select_matrix((16, 32), lambda a, c: (c >> 3) * 4 + ((c & 7) >> 1) == a), dot(coarse, half))
+    b5 = onto(pick.rows4, times(coarse, pick.kept("lanes4")))
 
     row, lane = iota((16, LANES), 0), iota((16, LANES), 1)
     mask5 = number(lane < 32)
@@ -435,63 +553,36 @@
     e5 = u5 + mask5 * (OWN * p5 + BETA * beside5(p5))
     env.coarse_out(e5)
 
-    double = select_matrix((128, 128), lambda a, c: (a == (c >> 1)) & (c < 64))
-    wide = dot(select_matrix((32, 16), lambda a, c: (a >> 3) * 4 + ((a & 7) >> 1) == c), dot(e5, double))
+    wide = onto(pick.up_rows5, times(e5, pick.kept("up5")))
     c4 = rows_of(wide, 8)
     c4 = field_of(0, [c4[z // 2] for z in range(8)])
     q4 = minus_op4(p4, c4)
     v4 = correction4(q4)
     e4 = [u4(z) + c4(z) + v4(z) for z in range(8)]
 
-    own_y = select_matrix((128, 128), lambda a, c: (a == 8 * iy + (((c & 31) - 8) >> 1)) & (c < 64))
-    planes = right(e4, own_y)
+    planes = right(e4, pick.kept("up4"))
     wide = jnp.concatenate([planes[2 * k] + m.roll(planes[2 * k + 1], 64, 1) for k in range(4)], axis=1)
-    c3 = mask3 * dot(select_matrix((16, 8), lambda a, c: (a >> 1) == c), wide)
-    e3 = u3 + c3 + correction3(minus_op3(p3, c3))
-
-    spread = select_matrix((16, 16), lambda a, c: 2 * ix + ((a - 6) >> 1) == c)
-    tiles = lanes_of(dot(spread, e3))
+    c3 = mask3 * onto(pick.up_rows4, wide)
+    e3 = u3(0) + c3 + correction3(minus_op3(p3(0), c3))
+
+    tiles = lanes_of(onto(pick.up_rows3, e3))
     near = env.window([m.roll(tiles[z // 4], -32 * (z % 4), 1) for z in range(16)])
-    y_of = lambda c: jnp.where(c < 80, c, c - 128)
-    own_y = select_matrix(
-        (128, 128), lambda a, c: (a - 8 == (y_of(c) >> 1)) & (a < 32) & (y_of(c) < 36) & (y_of(c) >= -4))
-    near = right(near, own_y)
-    c2 = field_of(-4, [near[(z >> 1) + 2] for z in range(-4, 8)])
-
-    def window(level, planes, tag, rows, row_off, lo, own_y, at_low, at_high):
-        mask = m.mask(level, rows, row_off, LANES, own_y)
-        before = m.unpack(env.shift_recv(tag + "+"), len(planes), at_low)
-        after = m.unpack(env.shift_recv(tag + "-"), len(planes), at_high)
-        return mask, field_of(lo, [
-            mask(lo + i) * (v + before[i] + after[i]) for i, v in enumerate(planes)
-        ])
-
-    mask2, b2 = window(2, b2w, "y2", 16, 6, -5, 32, 123, 30)
-    u2 = m.correction(b2, mask2, -4, 7)
-    p2 = m.minus_op(b2, u2, mask2, -3, 6)
-    v2 = m.correction(m.minus_op(p2, c2, mask2, -3, 6), mask2, -2, 5)
-    e2 = [u2(z) + mask2(z) * c2(z) + v2(z) for z in range(-2, 6)]
-
-    y_fine = lambda c: jnp.where(c < 96, c, c - 128)
-    own_y = select_matrix((128, 128), lambda a, c: y_of(a) == (y_fine(c) >> 1))
-    coarse = left(select_matrix((24, 16), lambda a, c: (a >> 1) + 2 == c), e2)
-    coarse = right(coarse, own_y)
-    c1 = field_of(-4, [coarse[(z >> 1) + 2] for z in range(-4, 12)])
-    mask1, b1 = window(1, b1w, "y1", 24, 8, -5, 64, 123, 62)
-    u1 = m.correction(b1, mask1, -4, 11)
-    p1 = m.minus_op(b1, u1, mask1, -3, 10)
-    v1 = m.correction(m.minus_op(p1, c1, mask1, -3, 10), mask1, -2, 9)
-    e1 = [u1(z) + mask1(z) * c1(z) + v1(z) for z in range(-2, 10)]
-
-    coarse = left(select_matrix((24, 24), lambda a, c: ((a - 4) >> 1) + 8 == c), e1)
-    coarse = right(coarse, select_matrix((128, 256), lambda a, c: a == (c >> 1)))
-    c0 = field_of(-4, [coarse[(z >> 1) + 2] for z in range(-4, 20)])
-    q0 = m.minus_op(p0, c0, mask0, -2, 17)
+    inner2, outer2 = widen(*halves(near), pick.kept("up3"), pick.kept("next3"))
+
+    v2 = m.correction(m.minus_op_of_coarse(p2, inner2, outer2, -2, mask2, -3, 6), mask2, -2, 5)
+    e2 = [u2(z) + inner2[(z >> 1) + 2] + v2(z) for z in range(-2, 6)]
+
+    inner1, outer1 = widen(*halves(left(pick.up_rows2, e2)), pick.kept("up2"), pick.kept("next2"))
+    v1 = m.correction(m.minus_op_of_coarse(p1, inner1, outer1, -2, mask1, -3, 10), mask1, -2, 9)
+    e1 = [u1(z) + inner1[(z >> 1) + 2] + v1(z) for z in range(-2, 10)]
+
+    inner0, outer0 = widen(*halves(left(pick.up_rows1, e1)), pick.kept("up1"), pick.kept("next1"))
+    q0 = m.minus_op_of_coarse(p0, inner0, outer0, -2, mask0, -2, 17)
     v0 = m.correction(q0, mask0, -1, 16)
-    left_over = m.minus_op(q0, v0, mask0, 0, 15)
+    left_over = m.minus_op(q0, v0, None, 0, 15)
     inner = lambda v: m.take_rows(v[:, :LANES], 4, 16)
     for z in range(16):
-        env.fine_out(z, x_own[z] + inner(u0(z) + c0(z) + v0(z)), inner(left_over(z)))
+        env.fine_out(z, s0(z) + inner(inner0[(z >> 1) + 2] + v0(z)), inner(left_over(z)))
 
 
 class KernelEnv:
@@ -500,9 +591,15 @@
         self.position = tuple(lax.axis_index(a) for a in ("gz", "gx", "gy"))
         self.at = dict(zip(("gz", "gx", "gy"), self.position))
         self.started = []
+        self.loads = [
+            pltpu.make_async_copy(refs["x_in"], refs["previous"], refs["load_sems"].at[0]),
+            pltpu.make_async_copy(refs["b_in"], refs["divergence"], refs["load_sems"].at[1]),
+        ]
+        for load in self.loads:
+            load.start()
         self.barrier = pltpu.get_barrier_semaphore()
-        for axis in ("gx", "gz", "gy"):
-            for d in range(1, RING):
+        for d in (4, 3, 5, 2, 6, 1, 7):
+            for axis in ("gx", "gy", "gz"):
                 pl.semaphore_signal(
                     self.barrier, inc=1, device_id={axis: self.peer(axis, d)}, device_id_type=pl.DeviceIdType.MESH)
 
@@ -511,6 +608,11 @@
 
     def roll(self, v, shift, axis):
         return pltpu.roll(v, shift, axis)
+
+    def load(self):
+        for load in self.loads:
+            load.wait()
+        return [[self.refs[n][16 * z:16 * z + 16] for z in range(16)] for n in ("previous", "divergence")]
 
     def row(self, planes, x):
         return self.refs["previous"][pl.ds(x, 16, stride=16), :]
@@ -566,13 +668,25 @@
 
     def window(self, planes):
         ref = self.refs["planes3"]
-        zero = jnp.zeros((16, LANES), jnp.float32)
+        zero = jnp.zeros((32, LANES), jnp.float32)
         for z in (0, 1, 18, 19):
             ref[z] = zero
         for z, v in enumerate(planes):
             ref[z + 2] = v
         return [ref[2 * self.position[0] + s] for s in range(6)]
 
+    def keep(self, name, lo, field):
+        ref = self.refs["kept_" + name]
+        for i in range(KEPT[name][0]):
+            ref[i] = field(lo + i)
+        return lambda z: ref[z - lo]
+
+    def keep_matrix(self, name, matrix):
+        self.refs["matrix_" + name][...] = matrix
+
+    def matrix(self, name):
+        return self.refs["matrix_" + name][...]
+
     def coarse_out(self, v):
         for z in range(4):
             self.refs["coarse"][z] = v[4 * z:4 * z + 4, :32]
@@ -581,9 +695,10 @@
         self.refs["pressure"][z] = pressure
         self.refs["residual"][z] = residual
 
-    def finish(self):
+    def flush(self):
         for copy in self.started:
             copy.wait_send()
+        self.started = []
 
 
 def scratch():
@@ -594,29 +709,24 @@
     for name, (_, rows) in GATHERS.items():
         shapes["out" + name] = pltpu.VMEM((rows, LANES), jnp.float32)
         shapes["in" + name] = pltpu.VMEM((RING, rows, LANES), jnp.float32)
+    for name, shape in KEPT.items():
+        shapes["kept_" + name] = pltpu.VMEM(shape, jnp.float32)
+    for name, shape in MATRICES.items():
+        shapes["matrix_" + name] = pltpu.VMEM(shape, jnp.bfloat16)
     shapes["previous"] = pltpu.VMEM((256, LANES), jnp.float32)
     shapes["divergence"] = pltpu.VMEM((256, LANES), jnp.float32)
     shapes["load_sems"] = pltpu.SemaphoreType.DMA((2,))
-    shapes["planes3"] = pltpu.VMEM((20, 16, LANES), jnp.float32)
+    shapes["planes3"] = pltpu.VMEM((20, 32, LANES), jnp.float32)
     shapes["shift_sems"] = pltpu.SemaphoreType.DMA((2, len(SHIFTS)))
     shapes["gather_sems"] = pltpu.SemaphoreType.DMA((2, len(GATHERS), RING))
     return shapes
 
 
 def kernel(names, divergence, previous, pressure, residual, coarse, *buffers):
-    refs = dict(zip(names, buffers), pressure=pressure, residual=residual, coarse=coarse)
-    loads = [
-        pltpu.make_async_copy(previous, refs["previous"], refs["load_sems"].at[0]),
-        pltpu.make_async_copy(divergence, refs["divergence"], refs["load_sems"].at[1]),
-    ]
-    for load in loads:
-        load.start()
+    refs = dict(zip(names, buffers), x_in=previous, b_in=divergence, pressure=pressure, residual=residual, coarse=coarse)
     env = KernelEnv(refs)
-    for load in loads:
-        load.wait()
-    planes = lambda name: [refs[name][16 * z:16 * z + 16] for z in range(16)]
-    cycle(env, planes("previous"), planes("divergence"))
-    env.finish()
+    cycle(env)
+    env.flush()
 
 
 def store_kernel(*refs):

time: 38.8 us -> 38 us (0.979)
  Pallas kernels: 38 us -> 37.2 us
    pallas_call x1, Pallas kernels: 37.3 us -> 36.5 us  [body(): pl.pallas_call(functools.partial(kernel, tuple(shapes)), out_shape=outs,...]
where the time goes in v3:
time: 38 us; the launch traced here: 37.8 us
  Pallas kernels  37.2 us (98%)
  between operations  0.64 us (2%)
    pallas_call x1, Pallas kernels, body(): pl.pallas_call(functools.partial(kernel, tuple(shapes)), out_shape=outs,...  36.5 us

profile of v3, /device:TPU:1, one launch (start us, length us, event | category | flops | bytes accessed | tf_op | source)
XLA Modules:
  0.0 37.8 jit_solution(13560199098611963131)
XLA Ops:
  0.6 36.5 %cycle.1 = (f32[16,16,128]{2,1,0:T(8,128)S(1)}, f32[16,16,128]{2,1,0:T(8,128)S(1)}, f32[4,4,32]{2,1,0:T(4,128)S(1)}) custom-call(f32[256,128]{1,0:T(8,128)} %bitcast.2, f32[256,128]{1,0:T(8,128)} %bitcast.3), custom_call_target="tpu_custom_call" | custom-call | tf_op jit(solution)/shard_map/cycle/pallas_call | solution.py:746
  37.1 0.7 %store.1 = (f32[16,16,128]{2,1,0:T(8,128)}, f32[16,16,128]{2,1,0:T(8,128)}, f32[4,4,32]{2,1,0:T(4,128)}) custom-call(f32[16,16,128]{2,1,0:T(8,128)S(1)} %get-tuple-element.6.refs_0_, f32[16,16,128]{2,1,0:T(8,128)S(1)} %get-tuple-element.7.refs_1_, f32[4,4,32]{2,1,0:T(4,128)S(1)} %get-tuple-element.8.refs_2_), custom_call_target="tpu_custom_call" | custom-call | tf_op jit(solution)/shard_map/store/pallas_call | solution.py:756

commit v4 on v3

--- a/solution.py
+++ b/solution.py
@@ -46,6 +46,7 @@
 MATRICES = {
     "lanes3": (512, 128), "lanes4": (128, 128), "up5": (128, 128), "up4": (128, 128), "up3": (128, 128),
     "up2": (128, 128), "up1": (128, 256), "next3": (128, 128), "next2": (128, 128), "next1": (128, 256),
+    "block4": (128, 128), "block3": (192, 128), "block2": (384, 128), "block1": (576, 384),
 }
 
 
@@ -75,6 +76,9 @@
 
 def onto(matrix, v):
     high, low = parts_of(v)
+    if v.shape[1] == LANES:
+        both = product(matrix, jnp.concatenate([high, low], axis=1))
+        return both[:, :LANES] + both[:, LANES:]
     return product(matrix, high) + product(matrix, low)
 
 
@@ -98,18 +102,24 @@
     return lanes_of(onto(matrix, jnp.concatenate(planes, axis=1)))
 
 
-def widen(own, beside, rows, up, following):
-    (own_high, own_low), (beside_high, beside_low) = parts_of(own), parts_of(beside)
-    join = lambda a, b: jnp.concatenate([a, b], axis=1)
-    inner = product(join(own_high, own_low), jnp.concatenate([up, up], axis=0))
-    both = jnp.concatenate([up, following], axis=0)
-    outer = product(join(beside_high, own_high), both) + product(join(beside_low, own_low), both)
-    return rows_of(inner, rows), rows_of(outer, rows)
-
-
-def halves(planes):
-    rows = planes[0].shape[0] // 2
-    return jnp.concatenate([v[:rows] for v in planes], axis=0), jnp.concatenate([v[rows:] for v in planes], axis=0), rows
+def twice(matrix):
+    return jnp.concatenate([matrix, matrix], axis=0)
+
+
+def spread_rows(planes, block):
+    stacked = jnp.concatenate(planes, axis=0)
+    missing = block.shape[1] - stacked.shape[0]
+    if missing:
+        stacked = jnp.concatenate([stacked, jnp.zeros((missing, LANES), jnp.float32)], axis=0)
+    return product(block, jnp.concatenate(parts_of(stacked), axis=1)).astype(jnp.bfloat16)
+
+
+def widen(planes, rows, block, up, following):
+    both = spread_rows(planes, block)
+    half = both.shape[0] // 2
+    own, beside = both[:half], both[half:]
+    outer = product(beside, twice(up)) + product(own, twice(following))
+    return rows_of(product(own, twice(up)), rows), rows_of(outer, rows)
 
 
 def total(terms):
@@ -231,11 +241,20 @@
         y_fine = lambda c: jnp.where(c < 96, c, c - 128)
         side = lambda c: 2 * (c & 1) - 1
 
-        def up_rows(rows, depth, coarse):
-            fine = lambda a: jnp.where(a >= rows, a - rows, a)
-            return select_matrix((2 * rows, depth), lambda a, c: (
-                coarse(fine(a)) + jnp.where(a >= rows, side(fine(a)), 0) == c))
-
+        def blocks(rows, depth, count, coarse, kinds=2):
+            shape = (rows, -(-count * depth // LANES) * LANES)
+            fine, column = iota(shape, 0), iota(shape, 1)
+            out = []
+            for kind in range(kinds):
+                want = coarse(fine) + kind * side(fine)
+                gap = column - jnp.where((want >= 0) & (want < depth), want, 4096)
+                out += [number(gap == depth * k) for k in range(count)]
+            return jnp.concatenate(out, axis=0).astype(jnp.bfloat16)
+
+        env.keep_matrix("block4", blocks(16, 8, 8, lambda a: a >> 1, 1))
+        env.keep_matrix("block3", blocks(16, 16, 6, lambda a: 2 * ix + ((a - 6) >> 1)))
+        env.keep_matrix("block2", blocks(24, 16, 8, lambda a: (a >> 1) + 2))
+        env.keep_matrix("block1", blocks(24, 24, 12, lambda a: ((a - 4) >> 1) + 8))
         hits = {
             "lanes3": lambda a, c: 16 * (a >> 6) + ((a & 31) >> 1) == c,
             "lanes4": lambda a, c: ((a >> 1) == c) & (a < 64),
@@ -255,10 +274,6 @@
         self.env = env
         self.rows4 = select_matrix((16, 32), lambda a, c: (c >> 3) * 4 + ((c & 7) >> 1) == a)
         self.up_rows5 = select_matrix((32, 16), lambda a, c: (a >> 3) * 4 + ((a & 7) >> 1) == c)
-        self.up_rows4 = select_matrix((16, 8), lambda a, c: (a >> 1) == c)
-        self.up_rows3 = up_rows(16, 16, lambda a: 2 * ix + ((a - 6) >> 1))
-        self.up_rows2 = up_rows(24, 16, lambda a: (a >> 1) + 2)
-        self.up_rows1 = up_rows(24, 24, lambda a: ((a - 4) >> 1) + 8)
 
     def kept(self, name):
         return self.env.matrix(name)
@@ -381,10 +396,6 @@
     env.shift_send("z1+", b1x[5:])
     env.shift_send("z1-", b1x[:7])
 
-    r0w = env.shift_recv("z0+") + r0x + env.shift_recv("z0-")
-    env.shift_send("y0+", m.pack(r0w, 124, 4))
-    env.shift_send("y0-", m.pack(r0w, 0, 4))
-
     parts = env.gather_recv("gz3")
     lane = iota((16, LANES), 1)
     tiles = []
@@ -428,6 +439,10 @@
     env.shift_send("y3+", [squeeze(19)])
     env.shift_send("y3-", [squeeze(6)])
 
+    r0w = env.shift_recv("z0+") + r0x + env.shift_recv("z0-")
+    env.shift_send("y0+", m.pack(r0w, 124, 4))
+    env.shift_send("y0-", m.pack(r0w, 0, 4))
+
     got = {d: env.shift_recv("z2%+d" % d) for d in (1, -1, 2, -2)}
     keep = m.slots(16, 126, 40)
 
@@ -466,47 +481,25 @@
     env.shift_send("y1+", m.pack(b1w, 59))
     env.shift_send("y1-", m.pack(b1w, 126))
 
+    kept = {}
+    before0, after0 = env.shift_recv("y0+"), env.shift_recv("y0-")
+
+    def finest():
+        mask = m.mask(0, 24, 4, 256, 128)
+        low, high = m.unpack(before0, 24, 124, 4), m.unpack(after0, 24, 0, 4)
+        r = field_of(-4, [
+            mask(i - 4) * jnp.concatenate([v, low[i] + high[i]], axis=1) for i, v in enumerate(r0w)
+        ])
+        u = m.correction(r, mask, -3, 18)
+        kept["p0"] = env.keep("p0", -2, m.minus_op(r, u, None, -2, 17))
+        near_x = Field(0, 15, lambda z: x_own[z] + m.take_rows(u(z)[:, :LANES], 4, 16))
+        kept["s0"] = env.keep("s0", 0, near_x)
+
+    env.region(finest)
+
     mask0 = m.mask(0, 24, 4, 256, 128)
-    low = m.unpack(env.shift_recv("y0+"), 24, 124, 4)
-    high = m.unpack(env.shift_recv("y0-"), 24, 0, 4)
-    r0 = field_of(-4, [
-        mask0(i - 4) * jnp.concatenate([v, low[i] + high[i]], axis=1) for i, v in enumerate(r0w)
-    ])
-    u0 = m.correction(r0, mask0, -3, 18)
-    p0 = m.minus_op(r0, u0, None, -2, 17)
-    p0 = Field(-2, 17, env.keep("p0", -2, p0))
-    near_x = Field(0, 15, lambda z: x_own[z] + m.take_rows(u0(z)[:, :LANES], 4, 16))
-    s0 = env.keep("s0", 0, near_x)
-
-    before, after = env.shift_recv("y3+")[0], env.shift_recv("y3-")[0]
-    slot16 = lane16 & 31
-    low_slot, high_slot = number((slot16 >= 3) & (slot16 < 11)), number((slot16 >= 22) & (slot16 < 30))
-    b3w = mask3 * (b3s + jnp.concatenate([
-        low_slot * m.roll(before, 3 - 8 * q, 1) + high_slot * m.roll(after, 22 - 8 * q, 1) for q in range(4)
-    ], axis=1))
-    u3 = correction3(b3w)
-    p3 = minus_op3(b3w, u3)
-    early_u3, early_p3 = u3, p3
-    u3, p3 = env.keep("u3", 0, lambda z: early_u3), env.keep("p3", 0, lambda z: early_p3)
-
-    def window(level, planes, tag, rows, row_off, lo, own_y, at_low, at_high):
-        mask = m.mask(level, rows, row_off, LANES, own_y)
-        before = m.unpack(env.shift_recv(tag + "+"), len(planes), at_low)
-        after = m.unpack(env.shift_recv(tag + "-"), len(planes), at_high)
-        return mask, field_of(lo, [
-            mask(lo + i) * (v + before[i] + after[i]) for i, v in enumerate(planes)
-        ])
-
-    mask2, b2 = window(2, b2w, "y2", 16, 6, -5, 32, 123, 30)
-    u2 = m.correction(b2, mask2, -4, 7)
-    p2 = m.minus_op(b2, u2, None, -3, 6)
-    p2 = Field(-3, 6, env.keep("p2", -3, p2))
-    u2 = env.keep("u2", -2, u2)
-    mask1, b1 = window(1, b1w, "y1", 24, 8, -5, 64, 123, 62)
-    u1 = m.correction(b1, mask1, -4, 11)
-    p1 = m.minus_op(b1, u1, None, -3, 10)
-    p1 = Field(-3, 10, env.keep("p1", -3, p1))
-    u1 = env.keep("u1", -2, u1)
+    mask1 = m.mask(1, 24, 8, LANES, 64)
+    mask2 = m.mask(2, 16, 6, LANES, 32)
     env.flush()
 
     parts = env.gather_recv("gy4")
@@ -553,30 +546,61 @@
     e5 = u5 + mask5 * (OWN * p5 + BETA * beside5(p5))
     env.coarse_out(e5)
 
-    wide = onto(pick.up_rows5, times(e5, pick.kept("up5")))
+    sides = {tag: (env.shift_recv(tag + "+"), env.shift_recv(tag + "-")) for tag in ("y3", "y2", "y1")}
+
+    def window(level, planes, tag, rows, row_off, lo, own_y, at_low, at_high):
+        mask = m.mask(level, rows, row_off, LANES, own_y)
+        before = m.unpack(sides[tag][0], len(planes), at_low)
+        after = m.unpack(sides[tag][1], len(planes), at_high)
+        return mask, field_of(lo, [
+            mask(lo + i) * (v + before[i] + after[i]) for i, v in enumerate(planes)
+        ])
+
+    def coarser():
+        before, after = sides["y3"][0][0], sides["y3"][1][0]
+        slot16 = lane16 & 31
+        low_slot, high_slot = number((slot16 >= 3) & (slot16 < 11)), number((slot16 >= 22) & (slot16 < 30))
+        b = mask3 * (b3s + jnp.concatenate([
+            low_slot * m.roll(before, 3 - 8 * q, 1) + high_slot * m.roll(after, 22 - 8 * q, 1) for q in range(4)
+        ], axis=1))
+        u = correction3(b)
+        kept["u3"], kept["p3"] = env.keep("u3", 0, lambda z: u), env.keep("p3", 0, lambda z: minus_op3(b, u))
+        mask, b2 = window(2, b2w, "y2", 16, 6, -5, 32, 123, 30)
+        u2 = m.correction(b2, mask, -4, 7)
+        kept["p2"] = env.keep("p2", -3, m.minus_op(b2, u2, None, -3, 6))
+        kept["u2"] = env.keep("u2", -2, u2)
+        mask, b1 = window(1, b1w, "y1", 24, 8, -5, 64, 123, 62)
+        u1 = m.correction(b1, mask, -4, 11)
+        kept["p1"] = env.keep("p1", -3, m.minus_op(b1, u1, None, -3, 10))
+        kept["u1"] = env.keep("u1", -2, u1)
+
+    coarser()
+    s0, u1, u2, u3, p3 = (kept[name] for name in ("s0", "u1", "u2", "u3", "p3"))
+    p0, p1, p2 = Field(-2, 17, kept["p0"]), Field(-3, 10, kept["p1"]), Field(-3, 6, kept["p2"])
+
+    wide = product(spread_rows([e5], pick.up_rows5), twice(pick.kept("up5")))
     c4 = rows_of(wide, 8)
     c4 = field_of(0, [c4[z // 2] for z in range(8)])
     q4 = minus_op4(p4, c4)
     v4 = correction4(q4)
     e4 = [u4(z) + c4(z) + v4(z) for z in range(8)]
 
-    planes = right(e4, pick.kept("up4"))
-    wide = jnp.concatenate([planes[2 * k] + m.roll(planes[2 * k + 1], 64, 1) for k in range(4)], axis=1)
-    c3 = mask3 * onto(pick.up_rows4, wide)
+    planes = rows_of(product(spread_rows(e4, pick.kept("block4")), twice(pick.kept("up4"))), 16)
+    c3 = mask3 * jnp.concatenate([planes[2 * k] + m.roll(planes[2 * k + 1], 64, 1) for k in range(4)], axis=1)
     e3 = u3(0) + c3 + correction3(minus_op3(p3(0), c3))
 
-    tiles = lanes_of(onto(pick.up_rows3, e3))
+    tiles = lanes_of(e3)
     near = env.window([m.roll(tiles[z // 4], -32 * (z % 4), 1) for z in range(16)])
-    inner2, outer2 = widen(*halves(near), pick.kept("up3"), pick.kept("next3"))
+    inner2, outer2 = widen(near, 16, pick.kept("block3"), pick.kept("up3"), pick.kept("next3"))
 
     v2 = m.correction(m.minus_op_of_coarse(p2, inner2, outer2, -2, mask2, -3, 6), mask2, -2, 5)
     e2 = [u2(z) + inner2[(z >> 1) + 2] + v2(z) for z in range(-2, 6)]
 
-    inner1, outer1 = widen(*halves(left(pick.up_rows2, e2)), pick.kept("up2"), pick.kept("next2"))
+    inner1, outer1 = widen(e2, 24, pick.kept("block2"), pick.kept("up2"), pick.kept("next2"))
     v1 = m.correction(m.minus_op_of_coarse(p1, inner1, outer1, -2, mask1, -3, 10), mask1, -2, 9)
     e1 = [u1(z) + inner1[(z >> 1) + 2] + v1(z) for z in range(-2, 10)]
 
-    inner0, outer0 = widen(*halves(left(pick.up_rows1, e1)), pick.kept("up1"), pick.kept("next1"))
+    inner0, outer0 = widen(e1, 24, pick.kept("block1"), pick.kept("up1"), pick.kept("next1"))
     q0 = m.minus_op_of_coarse(p0, inner0, outer0, -2, mask0, -2, 17)
     v0 = m.correction(q0, mask0, -1, 16)
     left_over = m.minus_op(q0, v0, None, 0, 15)
@@ -668,12 +692,15 @@
 
     def window(self, planes):
         ref = self.refs["planes3"]
-        zero = jnp.zeros((32, LANES), jnp.float32)
+        zero = jnp.zeros((16, LANES), jnp.float32)
         for z in (0, 1, 18, 19):
             ref[z] = zero
         for z, v in enumerate(planes):
             ref[z + 2] = v
         return [ref[2 * self.position[0] + s] for s in range(6)]
+
+    def region(self, work):
+        pl.when(self.position[0] < RING)(work)
 
     def keep(self, name, lo, field):
         ref = self.refs["kept_" + name]
@@ -716,7 +743,7 @@
     shapes["previous"] = pltpu.VMEM((256, LANES), jnp.float32)
     shapes["divergence"] = pltpu.VMEM((256, LANES), jnp.float32)
     shapes["load_sems"] = pltpu.SemaphoreType.DMA((2,))
-    shapes["planes3"] = pltpu.VMEM((20, 32, LANES), jnp.float32)
+    shapes["planes3"] = pltpu.VMEM((20, 16, LANES), jnp.float32)
     shapes["shift_sems"] = pltpu.SemaphoreType.DMA((2, len(SHIFTS)))
     shapes["gather_sems"] = pltpu.SemaphoreType.DMA((2, len(GATHERS), RING))
     return shapes

time: 38 us -> 36.4 us (0.958)
  Pallas kernels: 37.2 us -> 35.7 us
    pallas_call x1, Pallas kernels: 36.5 us -> 34.9 us  [body(): pl.pallas_call(functools.partial(kernel, tuple(shapes)), out_shape=outs,...]
where the time goes in v4:
time: 36.4 us; the launch traced here: 36.3 us
  Pallas kernels  35.7 us (98%)
  between operations  0.64 us (2%)
    pallas_call x1, Pallas kernels, body(): pl.pallas_call(functools.partial(kernel, tuple(shapes)), out_shape=outs,...  34.9 us
    pallas_call x1, Pallas kernels, body(): pl.pallas_call(store_kernel, out_shape=outs, in_specs=[vmem, vmem, vmem],...  0.73 us

profile of v4, /device:TPU:1, one launch (start us, length us, event | category | flops | bytes accessed | tf_op | source)
XLA Modules:
  0.0 36.3 jit_solution(4734816367042944172)
XLA Ops:
  0.6 34.9 %cycle.1 = (f32[16,16,128]{2,1,0:T(8,128)S(1)}, f32[16,16,128]{2,1,0:T(8,128)S(1)}, f32[4,4,32]{2,1,0:T(4,128)S(1)}) custom-call(f32[256,128]{1,0:T(8,128)} %bitcast.2, f32[256,128]{1,0:T(8,128)} %bitcast.3), custom_call_target="tpu_custom_call" | custom-call | tf_op jit(solution)/shard_map/cycle/pallas_call | solution.py:773
  35.6 0.7 %store.1 = (f32[16,16,128]{2,1,0:T(8,128)}, f32[16,16,128]{2,1,0:T(8,128)}, f32[4,4,32]{2,1,0:T(4,128)}) custom-call(f32[16,16,128]{2,1,0:T(8,128)S(1)} %get-tuple-element.6.refs_0_, f32[16,16,128]{2,1,0:T(8,128)S(1)} %get-tuple-element.7.refs_1_, f32[4,4,32]{2,1,0:T(4,128)S(1)} %get-tuple-element.8.refs_2_), custom_call_target="tpu_custom_call" | custom-call | tf_op jit(solution)/shard_map/store/pallas_call | solution.py:783

commit v5 on v4

--- a/solution.py
+++ b/solution.py
@@ -234,6 +234,11 @@
         self.halve_rows = select_matrix((8, 16), lambda a, c: (c >> 1) == a)
         self.lanes2 = select_matrix((128, 128), lambda a, c: (jnp.where(a < 80, a, a - 128) >> 1) + 2 == c, 0.5)
         self.ix, self.iy = ix, iy
+
+    def small(self, env):
+        self.env = env
+        self.rows4 = select_matrix((16, 32), lambda a, c: (c >> 3) * 4 + ((c & 7) >> 1) == a)
+        self.up_rows5 = select_matrix((32, 16), lambda a, c: (a >> 3) * 4 + ((a & 7) >> 1) == c)
 
     def rest(self, env):
         ix, iy = self.ix, self.iy
@@ -271,9 +276,6 @@
         for name, hit in hits.items():
             value = 0.5 if name.startswith("lanes") else 1.0
             env.keep_matrix(name, select_matrix(MATRICES[name], hit, value))
-        self.env = env
-        self.rows4 = select_matrix((16, 32), lambda a, c: (c >> 3) * 4 + ((c & 7) >> 1) == a)
-        self.up_rows5 = select_matrix((32, 16), lambda a, c: (a >> 3) * 4 + ((a & 7) >> 1) == c)
 
     def kept(self, name):
         return self.env.matrix(name)
@@ -355,13 +357,14 @@
     env.shift_send("x0+", [two(half(r_own[2 * i][8:]), r_own[2 * i + 1][8:]) for i in range(8)])
     env.shift_send("x0-", [two(r_own[2 * i][:8], half(r_own[2 * i + 1][:8])) for i in range(8)])
 
-    pick.rest(env)
+    pick.small(env)
 
     parts = env.gather_recv("gx3")
     wide = total([m.place_rows(v, 2 * k, 24) for k, v in enumerate(parts)])
     b3x = m.take_rows(wide, 2, 16)
 
     env.gather_send("gz3", b3x)
+    env.region(lambda: pick.rest(env))
 
     before, after = env.shift_recv("x0+"), env.shift_recv("x0-")
     r0x = []
@@ -619,13 +622,14 @@
             pltpu.make_async_copy(refs["x_in"], refs["previous"], refs["load_sems"].at[0]),
             pltpu.make_async_copy(refs["b_in"], refs["divergence"], refs["load_sems"].at[1]),
         ]
-        for load in self.loads:
-            load.start()
         self.barrier = pltpu.get_barrier_semaphore()
         for d in (4, 3, 5, 2, 6, 1, 7):
             for axis in ("gx", "gy", "gz"):
                 pl.semaphore_signal(
                     self.barrier, inc=1, device_id={axis: self.peer(axis, d)}, device_id_type=pl.DeviceIdType.MESH)
+            if d == 4:
+                for load in self.loads:
+                    load.start()
 
     def peer(self, axis, d):
         return lax.rem(self.at[axis] + (d + RING), RING)

time: 36.4 us -> 36.5 us (level)
  no operation moved by 1% of the time
where the time goes in v5:
time: 36.5 us; the launch traced here: 36.4 us
  Pallas kernels  35.8 us (98%)
  between operations  0.64 us (2%)
    pallas_call x1, Pallas kernels, body(): pl.pallas_call(functools.partial(kernel, tuple(shapes)), out_shape=outs,...  35 us

profile of v5, /device:TPU:1, one launch (start us, length us, event | category | flops | bytes accessed | tf_op | source)
XLA Modules:
  0.0 36.4 jit_solution(8455509354483943219)
XLA Ops:
  0.6 35.0 %cycle.1 = (f32[16,16,128]{2,1,0:T(8,128)S(1)}, f32[16,16,128]{2,1,0:T(8,128)S(1)}, f32[4,4,32]{2,1,0:T(4,128)S(1)}) custom-call(f32[256,128]{1,0:T(8,128)} %bitcast.2, f32[256,128]{1,0:T(8,128)} %bitcast.3), custom_call_target="tpu_custom_call" | custom-call | tf_op jit(solution)/shard_map/cycle/pallas_call | solution.py:777
  35.7 0.7 %store.1 = (f32[16,16,128]{2,1,0:T(8,128)}, f32[16,16,128]{2,1,0:T(8,128)}, f32[4,4,32]{2,1,0:T(4,128)}) custom-call(f32[16,16,128]{2,1,0:T(8,128)S(1)} %get-tuple-element.6.refs_0_, f32[16,16,128]{2,1,0:T(8,128)S(1)} %get-tuple-element.7.refs_1_, f32[4,4,32]{2,1,0:T(4,128)S(1)} %get-tuple-element.8.refs_2_), custom_call_target="tpu_custom_call" | custom-call | tf_op jit(solution)/shard_map/store/pallas_call | solution.py:787
